TPU v7x, 32 devices: a whole 2x2x4 slice. The times are simulated.
32 devices in a mesh: ctx: 16 (over z, y, x), fsdp: 2 (over core).
Axes of the slice: x: 2, y: 2, z: 4, core: 2. Of those that a mesh axis runs over, the one named last changes fastest.
Arguments:
- tokens: bfloat16 [2, 2048, 768], P('fsdp', 'ctx'), may hold values from -6 to 6
- qkv_weight: bfloat16 [3, 768, 768], P(None, 'fsdp'), may hold values from -0.21875 to 0.21875
- out_weight: bfloat16 [768, 768], P('fsdp'), may hold values from -6 to 6
- bias_table: float32 [32, 12], replicated, may hold values from -4 to 4
- norm_gain: bfloat16 [2, 768], P(None, 'fsdp'), may hold values from 0.5 to 1.5
- router_weight: bfloat16 [768, 32], P('fsdp'), may hold values from -0.15625 to 0.15625
- expert_in: bfloat16 [32, 768, 3072], P('ctx', 'fsdp'), may hold values from -0.21875 to 0.21875
- expert_out: bfloat16 [32, 3072, 768], P('ctx', 'fsdp'), may hold values from -6 to 6
- expert_ids: int32 [2, 2048], P('fsdp', 'ctx'), may hold values from 0 to 31, as said below
- slot_ids: int32 [2, 2048], P('fsdp', 'ctx'), may hold values from 0 to 7, as said below
- bucket_table: int32 [4095], replicated, may hold values from 0 to 31, as said below
- grad_out: bfloat16 [2, 2048, 768], P('fsdp', 'ctx'), may hold values from -6 to 6
Outputs:
- layer_out: bfloat16 [2, 2048, 768], P('fsdp', 'ctx')
- grad_tokens: float32 [2, 2048, 768], P('fsdp', 'ctx')
- grad_qkv: float32 [3, 768, 768], P(None, 'fsdp')
- grad_out_weight: float32 [768, 768], P('fsdp')
- grad_bias: float32 [32, 12], P('fsdp')
- grad_gain: float32 [2, 768], P(None, 'fsdp')
- grad_router: float32 [768, 32], P('fsdp')
- grad_expert_in: float32 [32, 768, 3072], P('ctx', 'fsdp')
- grad_expert_out: float32 [32, 3072, 768], P('ctx', 'fsdp')
Inputs may be any that keep to these rules, and one draw needn't show every extreme that they name: `expert_ids`: the tokens of one device name each expert at most 8 times, and some expert exactly 8 times. `slot_ids`: among one device's tokens, two that name the same expert never share a slot. `bucket_table`: entry 2047 + r holds the bucket of the offset r = key place - query place.
All inputs are finite; a program needn't handle non-finite values.
Results may differ from a plain program's by a relative error of at most 0.028.
Values may be sent and summed in bfloat16 or wider, within the bound.
A program may use at most 192 MiB of HBM per device.

v0:
```python
import jax
import jax.numpy as jnp
from jax import lax
from jax.sharding import PartitionSpec as P

HEADS = 12


epsilon = 1e-06
block_limit = 512


def gelu_curve(values):
    return jax.nn.gelu(values, approximate=True)


def rms_apply(values, gain_vec):
    factor = lax.rsqrt(jnp.mean(values * values, axis=-1, keepdims=True) + epsilon)
    return (values * factor * gain_vec, factor)


def rms_grad(values, factor, gain_vec, upstream):
    scaled = upstream * gain_vec
    inner_mean = jnp.mean(scaled * values, axis=-1, keepdims=True)
    return (
        factor * scaled - values * factor * factor * factor * inner_mean,
        jnp.sum(upstream * values * factor, axis=0),
    )


def split_heads(values, head_count):
    return values.reshape(values.shape[0], head_count, values.shape[1] // head_count)


def join_heads(values):
    return jnp.transpose(values, (1, 0, 2)).reshape(
        values.shape[1], values.shape[0] * values.shape[2]
    )


def bucket_marks(bias_table, bucket_table, query_first, key_first, query_count, key_count):
    centre = (bucket_table.shape[0] - 1) // 2
    span = query_count + key_count - 1
    start = key_first - query_first - (query_count - 1) + centre
    window = lax.dynamic_slice_in_dim(bucket_table, start, span, 0)
    return (window[:, None] == jnp.arange(bias_table.shape[0], dtype=jnp.int32)[None, :]).astype(
        jnp.float32
    )


def bias_line(bias_table, marks):
    return jnp.dot(
        marks, bias_table, precision=lax.Precision.HIGHEST, preferred_element_type=jnp.float32
    ).T


def spread_line(line, query_count, key_count):
    head_count, span = line.shape
    shifted = jnp.roll(line, -(query_count - 1), axis=1)
    tiled = jnp.tile(shifted, (1, query_count))[:, : query_count * (span - 1)]
    return tiled.reshape(head_count, query_count, span - 1)[:, :, :key_count]


def diagonal_sums(grid, span):
    head_count, query_count, key_count = grid.shape
    padded = jnp.pad(grid, ((0, 0), (0, 0), (0, span - 1 - key_count)))
    flat = jnp.pad(padded.reshape(head_count, query_count * (span - 1)), ((0, 0), (0, query_count)))
    folded = jnp.sum(flat.reshape(head_count, query_count, span), axis=1)
    return jnp.roll(folded, query_count - 1, axis=1)


def by_blocks(block_fn, carried, pieces):
    row_count = pieces[0].shape[0]
    turn_count = row_count // block_limit
    reshaped = tuple(
        (piece.reshape((turn_count, block_limit) + piece.shape[1:]) for piece in pieces)
    )

    def one_turn(running, scan_item):
        number, sliced = scan_item
        return (block_fn(running, sliced, number * block_limit), None)

    carried, _ = lax.scan(one_turn, carried, (jnp.arange(turn_count, dtype=jnp.int32), reshaped))
    return carried


def per_device(
    tokens,
    qkv_weight,
    out_weight,
    bias_table,
    norm_gain,
    router_weight,
    expert_in,
    expert_out,
    expert_ids,
    slot_ids,
    bucket_table,
    grad_out,
):
    head_count = HEADS
    qkv_full, out_full, gain_full, router_full = (
        lax.all_gather(qkv_weight, "fsdp", axis=1, tiled=True),
        lax.all_gather(out_weight, "fsdp", axis=0, tiled=True),
        lax.all_gather(norm_gain, "fsdp", axis=1, tiled=True),
        lax.all_gather(router_weight, "fsdp", axis=0, tiled=True),
    )
    in_full, outer_full = (
        lax.all_gather(expert_in, "fsdp", axis=1, tiled=True),
        lax.all_gather(expert_out, "fsdp", axis=1, tiled=True),
    )
    row_count = tokens.shape[1]
    model_width = tokens.shape[2]
    head_width = model_width // head_count
    expert_count = router_full.shape[1]
    capacity = max(2, 2 * row_count // expert_count)
    query_first = lax.axis_index("ctx") * row_count
    gains_float = gain_full.astype(jnp.float32)
    residual = tokens[0].astype(jnp.float32)
    normed_one, factor_one = rms_apply(residual, gains_float[0])
    normed_low = normed_one.astype(jnp.bfloat16)
    queries = jnp.dot(normed_low, qkv_full[0], preferred_element_type=jnp.float32).astype(
        jnp.bfloat16
    )
    keys_low = jnp.dot(normed_low, qkv_full[1], preferred_element_type=jnp.float32).astype(
        jnp.bfloat16
    )
    values_low = jnp.dot(normed_low, qkv_full[2], preferred_element_type=jnp.float32).astype(
        jnp.bfloat16
    )
    query_heads = split_heads(queries, head_count)
    key_heads = split_heads(keys_low, head_count)
    value_heads = split_heads(values_low, head_count)

    def forward_block(carried, pieces, first_row):
        running_max, row_total, weighted = carried
        key_part, value_part = pieces
        part_rows = key_part.shape[0]
        marks = bucket_marks(bias_table, bucket_table, query_first, first_row, row_count, part_rows)
        pos_bias = spread_line(bias_line(bias_table, marks), row_count, part_rows)
        scores = (
            jnp.einsum(
                "qhd,khd->hqk",
                query_heads,
                split_heads(key_part, head_count),
                preferred_element_type=jnp.float32,
            )
            * 0.125
            + pos_bias
        )
        new_max = jnp.maximum(running_max, jnp.max(scores, axis=-1))
        shrink = jnp.exp(running_max - new_max)
        exp_scores = jnp.exp(scores - new_max[:, :, None])
        row_total = row_total * shrink + jnp.sum(exp_scores, axis=-1)
        weighted = weighted * shrink[:, :, None] + jnp.einsum(
            "hqk,khd->hqd",
            exp_scores.astype(jnp.bfloat16),
            split_heads(value_part, head_count),
            preferred_element_type=jnp.float32,
        )
        return (new_max, row_total, weighted)

    def forward_fold(carried, pieces):
        return by_blocks(forward_block, carried, pieces)

    empty_state = (
        jnp.full((head_count, row_count), -jnp.inf, jnp.float32),
        jnp.zeros((head_count, row_count), jnp.float32),
        jnp.zeros((head_count, row_count, head_width), jnp.float32),
    )
    run_max, run_total, run_weighted = forward_fold(
        empty_state,
        (
            lax.all_gather(keys_low, "ctx", axis=0, tiled=True),
            lax.all_gather(values_low, "ctx", axis=0, tiled=True),
        ),
    )
    attended = run_weighted / run_total[:, :, None]
    mixed_low = join_heads(attended).astype(jnp.bfloat16)
    middle = residual + jnp.dot(mixed_low, out_full, preferred_element_type=jnp.float32)
    normed_two, factor_two = rms_apply(middle, gains_float[1])
    second_low = normed_two.astype(jnp.bfloat16)
    router_prob = jax.nn.softmax(
        jnp.dot(second_low, router_full, preferred_element_type=jnp.float32), axis=-1
    )
    owner = expert_ids[0]
    places = slot_ids[0]
    chosen = (owner[:, None] == jnp.arange(expert_count, dtype=jnp.int32)[None, :]).astype(
        jnp.float32
    )
    gates = jnp.sum(router_prob * chosen, axis=-1)
    send_rows = (
        jnp.zeros((capacity, expert_count, model_width), jnp.bfloat16)
        .at[places, owner]
        .set(second_low)
    )
    arrived = lax.all_to_all(send_rows, "ctx", split_axis=1, concat_axis=0, tiled=True)
    pre_act = jnp.einsum("ced,edf->cef", arrived, in_full, preferred_element_type=jnp.float32)
    active, gelu_pull = jax.vjp(gelu_curve, pre_act)
    active_low = active.astype(jnp.bfloat16)
    produced = jnp.einsum(
        "cef,efd->ced", active_low, outer_full, preferred_element_type=jnp.float32
    ).astype(jnp.bfloat16)
    returned = lax.all_to_all(produced, "ctx", split_axis=0, concat_axis=1, tiled=True)
    picked = returned[places, owner].astype(jnp.float32)
    layer_out = (middle + gates[:, None] * picked).astype(jnp.bfloat16)
    upstream = grad_out[0].astype(jnp.float32)
    gate_grad = jnp.sum(upstream * picked, axis=-1)
    grad_send = (
        jnp.zeros((capacity, expert_count, model_width), jnp.bfloat16)
        .at[places, owner]
        .set((gates[:, None] * upstream).astype(jnp.bfloat16))
    )
    grad_arrived = lax.all_to_all(grad_send, "ctx", split_axis=1, concat_axis=0, tiled=True)
    grad_outer = jnp.einsum(
        "cef,ced->efd", active_low, grad_arrived, preferred_element_type=jnp.float32
    )
    grad_active = jnp.einsum(
        "ced,efd->cef", grad_arrived, outer_full, preferred_element_type=jnp.float32
    )
    grad_pre = gelu_pull(grad_active)[0].astype(jnp.bfloat16)
    grad_inner = jnp.einsum("ced,cef->edf", arrived, grad_pre, preferred_element_type=jnp.float32)
    grad_rows = jnp.einsum(
        "cef,edf->ced", grad_pre, in_full, preferred_element_type=jnp.float32
    ).astype(jnp.bfloat16)
    grad_returned = lax.all_to_all(grad_rows, "ctx", split_axis=0, concat_axis=1, tiled=True)
    logit_grad = router_prob * (chosen - gates[:, None]) * gate_grad[:, None]
    second_float = second_low.astype(jnp.float32)
    router_grad = jnp.dot(
        second_float.T,
        logit_grad,
        precision=lax.Precision.HIGHEST,
        preferred_element_type=jnp.float32,
    )
    grad_second = grad_returned[places, owner].astype(jnp.float32) + jnp.dot(
        logit_grad,
        router_full.astype(jnp.float32).T,
        precision=lax.Precision.HIGHEST,
        preferred_element_type=jnp.float32,
    )
    grad_middle, gain_two_grad = rms_grad(middle, factor_two, gains_float[1], grad_second)
    grad_middle = grad_middle + upstream
    middle_low = grad_middle.astype(jnp.bfloat16)
    again_max, again_total, again_weighted = forward_fold(
        empty_state,
        (
            lax.all_gather(keys_low, "ctx", axis=0, tiled=True),
            lax.all_gather(values_low, "ctx", axis=0, tiled=True),
        ),
    )
    kept_out = again_weighted / again_total[:, :, None]
    kept_lse = again_max + jnp.log(again_total)
    kept_low = join_heads(kept_out).astype(jnp.bfloat16)
    grad_out_weight = jnp.dot(kept_low.T, middle_low, preferred_element_type=jnp.float32)
    grad_mixed = jnp.dot(middle_low, out_full.T, preferred_element_type=jnp.float32).astype(
        jnp.bfloat16
    )
    grad_heads = split_heads(grad_mixed, head_count)
    delta = jnp.einsum("qhd,hqd->hq", grad_heads.astype(jnp.float32), kept_out)
    lse_all, delta_all = (
        lax.all_gather(kept_lse.T, "ctx", axis=0, tiled=True),
        lax.all_gather(delta.T, "ctx", axis=0, tiled=True),
    )

    def query_block(carried, pieces, first_row):
        grad_query, grad_table = carried
        key_part, value_part = pieces
        part_rows = key_part.shape[0]
        marks = bucket_marks(bias_table, bucket_table, query_first, first_row, row_count, part_rows)
        pos_bias = spread_line(bias_line(bias_table, marks), row_count, part_rows)
        key_split = split_heads(key_part, head_count)
        scores = (
            jnp.einsum("qhd,khd->hqk", query_heads, key_split, preferred_element_type=jnp.float32)
            * 0.125
            + pos_bias
        )
        probability = jnp.exp(scores - kept_lse[:, :, None])
        prob_grad = jnp.einsum(
            "qhd,khd->hqk",
            grad_heads,
            split_heads(value_part, head_count),
            preferred_element_type=jnp.float32,
        )
        score_grad = (probability * (prob_grad - delta[:, :, None])).astype(jnp.bfloat16)
        grad_query = (
            grad_query
            + jnp.einsum("hqk,khd->hqd", score_grad, key_split, preferred_element_type=jnp.float32)
            * 0.125
        )
        line_grad = diagonal_sums(score_grad.astype(jnp.float32), marks.shape[0])
        grad_table = grad_table + jnp.dot(
            marks.T,
            line_grad.T,
            precision=lax.Precision.HIGHEST,
            preferred_element_type=jnp.float32,
        )
        return (grad_query, grad_table)

    def key_block(carried, pieces, first_row):
        grad_key, grad_value = carried
        query_part, upstream_part = pieces
        part_rows = query_part.shape[0]
        marks = bucket_marks(bias_table, bucket_table, first_row, query_first, part_rows, row_count)
        pos_bias = spread_line(bias_line(bias_table, marks), part_rows, row_count)
        lse_part = lax.dynamic_slice_in_dim(lse_all, first_row, part_rows, 0).T
        delta_part = lax.dynamic_slice_in_dim(delta_all, first_row, part_rows, 0).T
        query_split = split_heads(query_part, head_count)
        upstream_split = split_heads(upstream_part, head_count)
        scores = (
            jnp.einsum("qhd,khd->hqk", query_split, key_heads, preferred_element_type=jnp.float32)
            * 0.125
            + pos_bias
        )
        probability = jnp.exp(scores - lse_part[:, :, None])
        grad_value = grad_value + jnp.einsum(
            "hqk,qhd->hkd",
            probability.astype(jnp.bfloat16),
            upstream_split,
            preferred_element_type=jnp.float32,
        )
        prob_grad = jnp.einsum(
            "qhd,khd->hqk", upstream_split, value_heads, preferred_element_type=jnp.float32
        )
        score_grad = (probability * (prob_grad - delta_part[:, :, None])).astype(jnp.bfloat16)
        grad_key = (
            grad_key
            + jnp.einsum(
                "hqk,qhd->hkd", score_grad, query_split, preferred_element_type=jnp.float32
            )
            * 0.125
        )
        return (grad_key, grad_value)

    head_zeros = jnp.zeros((head_count, row_count, head_width), jnp.float32)
    grad_query, grad_table = by_blocks(
        query_block,
        (head_zeros, jnp.zeros((bias_table.shape[0], head_count), jnp.float32)),
        (
            lax.all_gather(keys_low, "ctx", axis=0, tiled=True),
            lax.all_gather(values_low, "ctx", axis=0, tiled=True),
        ),
    )
    grad_key, grad_value = by_blocks(
        key_block,
        (head_zeros, head_zeros),
        (
            lax.all_gather(queries, "ctx", axis=0, tiled=True),
            lax.all_gather(grad_mixed, "ctx", axis=0, tiled=True),
        ),
    )
    projected_grads = (
        join_heads(grad_query).astype(jnp.bfloat16),
        join_heads(grad_key).astype(jnp.bfloat16),
        join_heads(grad_value).astype(jnp.bfloat16),
    )
    grad_qkv = jnp.stack(
        [
            jnp.dot(normed_low.T, single, preferred_element_type=jnp.float32)
            for single in projected_grads
        ]
    )
    grad_normed = jnp.dot(projected_grads[0], qkv_full[0].T, preferred_element_type=jnp.float32)
    grad_normed = grad_normed + jnp.dot(
        projected_grads[1], qkv_full[1].T, preferred_element_type=jnp.float32
    )
    grad_normed = grad_normed + jnp.dot(
        projected_grads[2], qkv_full[2].T, preferred_element_type=jnp.float32
    )
    grad_first, gain_one_grad = rms_grad(residual, factor_one, gains_float[0], grad_normed)
    grad_tokens = (grad_first + grad_middle)[None]
    gain_grads = jnp.stack([gain_one_grad, gain_two_grad])
    shards = (
        lax.psum_scatter(
            grad_qkv.astype(jnp.bfloat16), "fsdp", scatter_dimension=1, tiled=True
        ).astype(jnp.float32),
        lax.psum_scatter(
            grad_out_weight.astype(jnp.bfloat16), "fsdp", scatter_dimension=0, tiled=True
        ).astype(jnp.float32),
        lax.psum_scatter(
            grad_table.astype(jnp.bfloat16), "fsdp", scatter_dimension=0, tiled=True
        ).astype(jnp.float32),
        lax.psum_scatter(
            gain_grads.astype(jnp.bfloat16), "fsdp", scatter_dimension=1, tiled=True
        ).astype(jnp.float32),
        lax.psum_scatter(
            router_grad.astype(jnp.bfloat16), "fsdp", scatter_dimension=0, tiled=True
        ).astype(jnp.float32),
    )
    totals = lax.psum((shards[0], shards[1], shards[2], shards[3], shards[4]), "ctx")
    expert_sums = (
        lax.psum_scatter(
            grad_inner.astype(jnp.bfloat16), "fsdp", scatter_dimension=1, tiled=True
        ).astype(jnp.float32),
        lax.psum_scatter(
            grad_outer.astype(jnp.bfloat16), "fsdp", scatter_dimension=1, tiled=True
        ).astype(jnp.float32),
    )
    final_inner, final_outer = (expert_sums[0], expert_sums[1])
    return (
        layer_out[None],
        grad_tokens,
        totals[0],
        totals[1],
        totals[2],
        totals[3],
        totals[4],
        final_inner,
        final_outer,
    )


def solution(mesh):
    placed = (
        P("fsdp", "ctx", None),
        P(None, "fsdp", None),
        P("fsdp", None),
        P(),
        P(None, "fsdp"),
        P("fsdp", None),
        P("ctx", "fsdp", None),
        P("ctx", "fsdp", None),
        P("fsdp", "ctx"),
        P("fsdp", "ctx"),
        P(),
        P("fsdp", "ctx", None),
    )
    return jax.shard_map(
        per_device,
        mesh=mesh,
        in_specs=placed,
        out_specs=(
            P("fsdp", "ctx", None),
            P("fsdp", "ctx", None),
            P(None, "fsdp", None),
            P("fsdp", None),
            P("fsdp", None),
            P(None, "fsdp"),
            P("fsdp", None),
            P("ctx", "fsdp", None),
            P("ctx", "fsdp", None),
        ),
        check_vma=False,
    )
```

profile of v0, /device:TPU:0, one launch (start us, length us, event | category | flops | bytes accessed | tf_op | source)
XLA Modules:
  0.0 1475.7 jit_solution(1149334358030426465)
XLA Ops:
  11.7 13.3 all-gather.9.cloned.1.call-done
  33.6 63.5 %all-gather.13.cloned.1.call-done = bf16[2048,768]{1,0:T(8,128)(2,1)} async-done(((bf16[128,768]{1,0:T(8,128)(2,1)}), bf16[2048,768]{1,0:T(8,128)(2,1)}) %all-gather.13.cloned.1.call-update) | async-done | bytes 3145744 | tf_op jit(solution)/shard_map/all_gather | solution.py:175
  101.8 64.8 %all-gather.11.cloned.1.call-done = bf16[2048,768]{1,0:T(8,128)(2,1)} async-done(((bf16[128,768]{1,0:T(8,128)(2,1)}), bf16[2048,768]{1,0:T(8,128)(2,1)}) %all-gather.11.cloned.1.call-update) | async-done | bytes 3145744 | tf_op jit(solution)/shard_map/all_gather | solution.py:174
  171.2 148.8 %while.59 = (s32[]{:T(128)}, f32[12,128]{1,0:T(8,128)S(1)}, f32[12,128]{1,0:T(8,128)}, f32[12,128,64]{1,2,0:T(8,128)}, bf16[4,512,768]{1,2,0:T(8,128)(2,1)}, /*i...) while((s32[]{:T(128)}, f32[12,128]{1,0:T(8,128)S(1)}, ...), condition=%wide.region_4.5_spmd.clone, body=%wide.region_1.4_spmd.clone.sunk | while | flops 210106848 | bytes 68103472 | solution.py:83
  185.3 7.0 slice.236
  192.3 8.0 reshape.437
  230.0 7.2 reshape.437
  266.4 7.2 reshape.437
  302.8 7.2 reshape.437
  323.8 8.2 scatter_fusion
  338.1 11.9 all-to-all-done
  356.0 6.6 fusion.41
  372.9 12.3 all-to-all-done.1
  395.4 17.7 %scatter_fusion.1 = bf16[8,32,768]{2,1,0:T(8,128)(2,1)} fusion(bf16[8,32,768]{2,1,0:T(8,128)(2,1)} %broadcast.241, s32[128]{0:T(128)S(1)} %get-tuple-element.1223, bf16[128,768]{1,0:T(8,128)(2,1)} %get-tuple-element.1238), kind=kCustom, calls=%fused_computation.3 | custom fusion | bytes 590848 | tf_op jit(solution)/shard_map/scatter | solution.py:212
  414.5 16.9 %all_to_all.72 = bf16[8,32,768]{2,0,1:T(8,128)(2,1)S(1)} all-to-all(bf16[8,32,768]{2,0,1:T(8,128)(2,1)S(1)} %copy.149), channel_id=1, replica_groups=mesh['ctx'=16,'fsdp'=2] {'ctx'}, dimensions={1} | all-to-all | bytes 786432 | tf_op jit(solution)/shard_map/all_to_all | solution.py:214
  431.4 7.4 fusion.37
  442.5 14.9 %all_to_all.73 = bf16[128,2,768]{2,1,0:T(2,128)(2,1)S(1)} all-to-all(bf16[128,2,768]{2,1,0:T(2,128)(2,1)S(1)} %copy.151), channel_id=1, replica_groups=mesh['ctx'=16,'fsdp'=2] {'ctx'}, dimensions={0} | all-to-all | bytes 786432 | tf_op jit(solution)/shard_map/all_to_all | solution.py:226
  468.1 41.1 %all_gather.49 = f32[2048,12]{0,1:T(8,128)} all-gather(f32[128,12]{0,1:T(8,128)S(1)} %bitcast.329), channel_id=1, replica_groups=mesh['ctx'=16,'fsdp'=2] {'ctx'}, dimensions={0}, use_global_device_ids=true | all-gather | bytes 104448 | tf_op jit(solution)/shard_map/all_gather | solution.py:261
  513.7 253.3 %while.60 = (s32[]{:T(128)}, f32[12,128,64]{1,2,0:T(8,128)}, f32[32,12]{0,1:T(8,128)}, bf16[4,512,768]{1,2,0:T(8,128)(2,1)}, bf16[128,12,64]{0,2,1:T(8,128)(2,1)...) while((s32[]{:T(128)}, f32[12,128,64]{1,2,0:T(8,128)}, ...), condition=%wide.region_15.16_spmd.clone, body=%wide.region_13.15_spmd.clone.sunk | while | flops 314904768 | bytes 97403392 | solution.py:83
  548.1 7.2 reshape.439
  575.3 6.8 reshape.441
  607.6 7.2 reshape.439
  635.8 6.8 reshape.441
  668.1 7.2 reshape.439
  696.3 6.8 reshape.441
  728.6 7.2 reshape.439
  756.8 6.8 reshape.441
  772.1 38.5 %all_gather.51 = f32[2048,12]{0,1:T(8,128)} all-gather(f32[128,12]{0,1:T(8,128)S(1)} %bitcast.328), channel_id=1, replica_groups=mesh['ctx'=16,'fsdp'=2] {'ctx'}, dimensions={0}, use_global_device_ids=true | all-gather | bytes 104448 | tf_op jit(solution)/shard_map/all_gather | solution.py:262
  814.5 404.6 %while.61 = (s32[]{:T(128)}, f32[12,128,64]{1,2,0:T(8,128)}, f32[12,128,64]{1,2,0:T(8,128)S(1)}, bf16[4,512,768]{2,1,0:T(8,128)(2,1)}, bf16[128,12,64]{0,2,1:T(8...) while((s32[]{:T(128)}, f32[12,128,64]{1,2,0:T(8,128)}, ...), condition=%wide.region_17.18_spmd.clone, body=%wide.region_16.17_spmd.clone.sunk | while | flops 411622368 | bytes 134157320 | solution.py:83
  840.8 6.5 tile.66
  847.4 25.2 %tile.67 = f32[12,327168]{1,0:T(8,128)} reshape(f32[12,512,639]{2,1,0:T(8,128)} %tile.66) | data formatting | bytes 31408128 | tf_op jit(solution)/shard_map/while/body/eval_jaxpr/tile | solution.py:60
  872.5 15.7 %slice.247 = f32[12,326656]{1,0:T(8,128)} slice(f32[12,327168]{1,0:T(8,128)} %tile.67), slice={[0:12], [0:326656]} | slice | bytes 31358976 | tf_op jit(solution)/shard_map/while/body/eval_jaxpr/slice | solution.py:60
  888.3 31.9 %reshape.442 = f32[12,512,638]{2,1,0:T(8,128)} reshape(f32[12,326656]{1,0:T(8,128)} %slice.247) | data formatting | bytes 31358976 | tf_op jit(solution)/shard_map/while/body/eval_jaxpr/reshape | solution.py:61
  937.4 6.5 tile.66
  943.9 25.2 %tile.67 = f32[12,327168]{1,0:T(8,128)} reshape(f32[12,512,639]{2,1,0:T(8,128)} %tile.66) | data formatting | bytes 31408128 | tf_op jit(solution)/shard_map/while/body/eval_jaxpr/tile | solution.py:60
  969.0 15.7 %slice.247 = f32[12,326656]{1,0:T(8,128)} slice(f32[12,327168]{1,0:T(8,128)} %tile.67), slice={[0:12], [0:326656]} | slice | bytes 31358976 | tf_op jit(solution)/shard_map/while/body/eval_jaxpr/slice | solution.py:60
  984.8 31.9 %reshape.442 = f32[12,512,638]{2,1,0:T(8,128)} reshape(f32[12,326656]{1,0:T(8,128)} %slice.247) | data formatting | bytes 31358976 | tf_op jit(solution)/shard_map/while/body/eval_jaxpr/reshape | solution.py:61
  1034.0 6.5 tile.66
  1040.5 25.2 %tile.67 = f32[12,327168]{1,0:T(8,128)} reshape(f32[12,512,639]{2,1,0:T(8,128)} %tile.66) | data formatting | bytes 31408128 | tf_op jit(solution)/shard_map/while/body/eval_jaxpr/tile | solution.py:60
  1065.7 15.7 %slice.247 = f32[12,326656]{1,0:T(8,128)} slice(f32[12,327168]{1,0:T(8,128)} %tile.67), slice={[0:12], [0:326656]} | slice | bytes 31358976 | tf_op jit(solution)/shard_map/while/body/eval_jaxpr/slice | solution.py:60
  1081.4 31.9 %reshape.442 = f32[12,512,638]{2,1,0:T(8,128)} reshape(f32[12,326656]{1,0:T(8,128)} %slice.247) | data formatting | bytes 31358976 | tf_op jit(solution)/shard_map/while/body/eval_jaxpr/reshape | solution.py:61
  1130.6 6.5 tile.66
  1137.2 25.2 %tile.67 = f32[12,327168]{1,0:T(8,128)} reshape(f32[12,512,639]{2,1,0:T(8,128)} %tile.66) | data formatting | bytes 31408128 | tf_op jit(solution)/shard_map/while/body/eval_jaxpr/tile | solution.py:60
  1162.3 15.7 %slice.247 = f32[12,326656]{1,0:T(8,128)} slice(f32[12,327168]{1,0:T(8,128)} %tile.67), slice={[0:12], [0:326656]} | slice | bytes 31358976 | tf_op jit(solution)/shard_map/while/body/eval_jaxpr/slice | solution.py:60
  1178.1 31.9 %reshape.442 = f32[12,512,638]{2,1,0:T(8,128)} reshape(f32[12,326656]{1,0:T(8,128)} %slice.247) | data formatting | bytes 31358976 | tf_op jit(solution)/shard_map/while/body/eval_jaxpr/reshape | solution.py:61
  1249.6 204.3 %all-reduce.4 = (f32[3,384,768]{2,1,0:T(8,128)}, f32[384,768]{1,0:T(8,128)}, f32[16,12]{0,1:T(8,128)S(1)}, f32[2,384]{1,0:T(2,128)}, f32[384,32]{0,1:T(8,128)}) all-reduce(bf16[3,384,768]{2,1,0:T(8,128)(2,1)} %reduce-scatter.14.cloned.1.call-done, ...), channel_id=1, replica_groups=mesh['ctx'=16,'fsdp'=2] {'ctx'}, use_global_device_ids=true, to_apply=%region_20.21 | all-reduce | flops 1192896 | bytes 7157376 | tf_op jit(solution)/shard_map/psum | solution.py:389
  1454.6 6.8 convert_element_type.268
  1461.4 7.4 convert_element_type.266
  (533 shorter events, 475.6 us)
Async XLA Ops:
  7.2 20.3 %copy-start.11 = (bf16[1,128,768]{2,1,0:T(8,128)(2,1)S(1)}, bf16[1,128,768]{2,1,0:T(8,128)(2,1)}, u32[]{:S(2)}) copy-start(bf16[1,128,768]{2,1,0:T(8,128)(2,1)} %param.18) | copy-start | bytes 589828
  7.2 17.8 %all-gather.9.cloned.1.call-start = ((), (), s32[]{:S(2)}) async-start(), calls=%async_computation.11 | async-start | bytes 5308416 | tf_op jit(solution)/shard_map/all_gather | solution.py:103
  7.9 89.2 %all-gather.13.cloned.1.call-start = ((), (), s32[]{:S(2)}) async-start(), calls=%async_computation.13 | async-start | bytes 3342336 | tf_op jit(solution)/shard_map/all_gather | solution.py:175
  10.6 21.1 %copy-start.36 = (f32[768]{0:T(1024)}, f32[768]{0:T(1024)S(1)}, u32[]{:S(2)}) copy-start(f32[768]{0:T(1024)S(1)} %get-tuple-element.1141) | copy-start | bytes 9220
  11.7 20.1 %copy-start.40 = (f32[128]{0:T(128)}, f32[128]{0:T(128)S(1)}, u32[]{:S(2)}) copy-start(f32[128]{0:T(128)S(1)} %add_rsqrt_fusion.1) | copy-start | bytes 1540
  27.5 139.1 %all-gather.11.cloned.1.call-start = ((), (), s32[]{:S(2)}) async-start(), calls=%async_computation.12 | async-start | bytes 3342336 | tf_op jit(solution)/shard_map/all_gather | solution.py:174
  29.9 291.2 %all-gather.15.cloned.1.call-start = ((), (), s32[]{:S(2)}) async-start(), calls=%async_computation.14 | async-start | bytes 1769472 | tf_op jit(solution)/shard_map/all_gather | solution.py:104
  30.5 307.6 %all-gather.17.cloned.1.call-start = ((), (), s32[]{:S(2)}) async-start(), calls=%async_computation.15 | async-start | bytes 14155776 | tf_op jit(solution)/shard_map/all_gather | solution.py:109
  31.1 324.9 %all-gather.19.cloned.1.call-start = ((), (), s32[]{:S(2)}) async-start(), calls=%async_computation.16 | async-start | bytes 14155776 | tf_op jit(solution)/shard_map/all_gather | solution.py:110
  33.4 68.4 %copy-start.27 = (bf16[128,768]{1,0:T(8,128)(2,1)}, bf16[128,768]{1,0:T(8,128)(2,1)S(1)}, u32[]{:S(2)}) copy-start(bf16[128,768]{1,0:T(8,128)(2,1)S(1)} %convolution_convert_fusion.10) | copy-start | bytes 589828
  171.2 8.0 copy-start.48
  210.5 8.2 copy-start.48
  247.2 8.0 copy-start.48
  283.6 8.0 copy-start.48
  333.0 16.9 %all-to-all-start = ((bf16[8,32,768]{2,0,1:T(8,128)(2,1)}), bf16[8,32,768]{2,0,1:T(8,128)(2,1)S(1)}, u32[]{:S(2)}, u32[]{:S(2)}) async-start(bf16[8,32,768]{2,0,1:T(8,128)(2,1)} %copy.145), calls=%async_computation | async-start | bytes 786432 | tf_op jit(solution)/shard_map/all_to_all | solution.py:197
  337.3 477.2 %all-gather.21.cloned.1.call-start = ((), (), s32[]{:S(2)}) async-start(), calls=%async_computation.17 | async-start | bytes 3342336 | tf_op jit(solution)/shard_map/all_gather | solution.py:347
  356.0 75.4 %copy-start.3 = (f32[128,2,3072]{2,0,1:T(8,128)}, f32[128,2,3072]{2,0,1:T(8,128)S(1)}, u32[]{:S(2)}) copy-start(f32[128,2,3072]{2,0,1:T(8,128)S(1)} %convolution_bitcast_fusion.4) | copy-start | bytes 9437188
  363.8 21.4 %all-to-all-start.1 = ((bf16[128,2,768]{2,1,0:T(2,128)(2,1)}), bf16[128,2,768]{2,1,0:T(2,128)(2,1)}, u32[]{:S(2)}, u32[]{:S(2)}) async-start(bf16[128,2,768]{2,1,0:T(2,128)(2,1)} %copy.147), calls=%async_computation.1 | async-start | bytes 786432 | tf_op jit(solution)/shard_map/all_to_all | solution.py:204
  368.0 446.4 %all-gather.23.cloned.1.call-start = ((), (), s32[]{:S(2)}) async-start(), calls=%async_computation.18 | async-start | bytes 3342336 | tf_op jit(solution)/shard_map/all_gather | solution.py:348
  413.1 25.7 %slice-start.2 = ((s8[9437184]{0:T(1024)(128)(4,1)}), s8[4194304]{0:T(1024)(128)(4,1)S(1)}, s32[]{:S(2)}) async-start(s8[9437184]{0:T(1024)(128)(4,1)} %bitcast.299), calls=%async_computation.28 | async-start | bytes 8388608
  431.3 7.4 copy-start.25
  431.3 7.4 slice-start.3
  431.4 7.4 slice-start.4
  442.1 17.3 %copy-start.17 = (f32[128,768]{1,0:T(8,128)S(1)}, f32[128,768]{1,0:T(8,128)}, u32[]{:S(2)}) copy-start(f32[128,768]{1,0:T(8,128)} %copy-done.16) | copy-start | bytes 1179652
  442.1 19.3 %copy-start.24 = (bf16[128,768]{1,0:T(8,128)(2,1)S(1)}, bf16[128,768]{1,0:T(8,128)(2,1)}, u32[]{:S(2)}) copy-start(bf16[128,768]{1,0:T(8,128)(2,1)} %gather_fusion) | copy-start | bytes 589828
  457.4 5.8 copy-start.21
  459.4 8.7 copy-start.30
  461.4 50.7 %copy-start.23 = (bf16[12,128,64]{1,2,0:T(8,128)(2,1)S(1)}, bf16[12,128,64]{1,2,0:T(8,128)(2,1)}, u32[]{:S(2)}) copy-start(bf16[12,128,64]{1,2,0:T(8,128)(2,1)} %copy-done.22) | copy-start | bytes 589828
  463.2 50.4 %copy-start.14 = (f32[128,768]{1,0:T(8,128)}, f32[128,768]{1,0:T(8,128)S(1)}, u32[]{:S(2)}) copy-start(f32[128,768]{1,0:T(8,128)S(1)} %get-tuple-element.1235) | copy-start | bytes 1179652
  463.2 50.4 %copy-start.7 = (f32[12,128,64]{1,2,0:T(8,128)S(1)}, f32[12,128,64]{1,2,0:T(8,128)}, u32[]{:S(2)}) copy-start(f32[12,128,64]{1,2,0:T(8,128)} %get-tuple-element.769) | copy-start | bytes 1179652
  464.5 781.2 %reduce-scatter.26.cloned.1.call-start = ((), (), s32[]{:S(2)}) async-start(), calls=%async_computation.25 | async-start | bytes 294912
  511.0 735.9 %reduce-scatter.22.cloned.1.call-start = ((), (), s32[]{:S(2)}) async-start(), calls=%async_computation.23 | async-start | bytes 12288
  525.9 8.7 copy-start.33
  559.5 4.3 copy-start.1
  585.5 8.7 copy-start.33
  619.1 4.3 copy-start.1
  646.0 8.7 copy-start.33
  679.6 4.3 copy-start.1
  706.5 8.7 copy-start.33
  740.1 4.3 copy-start.1
  767.0 47.4 %copy-start.8 = (f32[12,128,64]{1,2,0:T(8,128)S(1)}, f32[12,128,64]{1,2,0:T(8,128)}, u32[]{:S(2)}) copy-start(f32[12,128,64]{1,2,0:T(8,128)} %custom-call.14) | copy-start | bytes 1179652
  772.0 475.6 %reduce-scatter.16.cloned.1.call-start = ((), (), s32[]{:S(2)}) async-start(), calls=%async_computation.20 | async-start | bytes 1769472 | tf_op jit(solution)/shard_map/reduce_scatter | solution.py:376
  811.8 436.7 %reduce-scatter.24.cloned.1.call-start = ((), (), s32[]{:S(2)}) async-start(), calls=%async_computation.24 | async-start | bytes 294912
  1219.1 5.7 copy-start.39
  1222.1 5.8 copy-start.20
  1227.9 21.6 %reduce-scatter.14.cloned.1.call-start = ((), (), s32[]{:S(2)}) async-start(), calls=%async_computation.19 | async-start | bytes 5308416 | tf_op jit(solution)/shard_map/reduce_scatter | solution.py:373
  1231.1 223.5 %reduce-scatter.20.cloned.1.call-start = ((), (), s32[]{:S(2)}) async-start(), calls=%async_computation.22 | async-start | bytes 14155776 | tf_op jit(solution)/shard_map/reduce_scatter | solution.py:394
  1238.5 222.9 %reduce-scatter.18.cloned.1.call-start = ((), (), s32[]{:S(2)}) async-start(), calls=%async_computation.21 | async-start | bytes 14155776 | tf_op jit(solution)/shard_map/reduce_scatter | solution.py:391
  (69 other events, 107.9 us)
Sparse Core Ops, SparseCore 0:
  9.6 15.3 all-gather.8
  27.8 69.2 all-gather.12
  99.9 66.6 all-gather.10
  168.0 7.7 all-gather.14
  177.1 21.5 all-gather.16
  200.1 21.3 all-gather.18
  340.9 73.3 all-gather.20
  464.6 66.6 all-gather.22
  533.5 6.0 reduce-scatter.25
  772.2 3.2 reduce-scatter.21
  812.0 6.4 reduce-scatter.15
  1228.0 5.3 reduce-scatter.23
  1236.3 12.5 reduce-scatter.13
  1251.6 18.9 reduce-scatter.19
  1273.3 19.0 reduce-scatter.17
where the time goes:
time: 1490 us; the launch traced here: 1480 us
  local copies, waits for them, and re-layouts  714 us (48%)
  blocking collectives  320 us (21%)
  waiting for transfers between devices  169 us (11%)
  matrix products  158 us (11%)
  other arithmetic  51.6 us (3%)
  loops' own time  39.3 us (3%)
  between operations  15 us (1%)
    psum x1, blocking collectives, per_device(): lax.psum((shards[0], shards[1], shards[2], shards[3], shards[4]), 'ctx')  204 us
    another operation x24, local copies, waits for them, and re-layouts, spread_line(): tiled = jnp.tile(shifted, (1, query_count))[:, :query_count * (span - 1)]  193 us
    reshape x12, local copies, waits for them, and re-layouts, spread_line(): return tiled.reshape(head_count, query_count, span - 1)[:, :, :key_count]  186 us
    slice x12, local copies, waits for them, and re-layouts, spread_line(): tiled = jnp.tile(shifted, (1, query_count))[:, :query_count * (span - 1)]  106 us
    all_gather x1, waiting for transfers between devices, per_device(): lax.all_gather(keys_low, 'ctx', axis=0, tiled=True)  64.8 us
    all_gather x1, waiting for transfers between devices, per_device(): lax.all_gather(values_low, 'ctx', axis=0, tiled=True)  63.5 us
    dynamic_slice x32, local copies, waits for them, and re-layouts, by_blocks(): lax.scan(one_turn, carried, (jnp.arange(turn_count, dtype=jnp.int32), res...  42.3 us
    all_gather x1, blocking collectives, per_device(): lax.all_gather(kept_lse.T, 'ctx', axis=0, tiled=True)  41.1 us
  transfers between devices with their start and end apart: 17, of which 5 were waited for; matrix products, arithmetic and copies ran while one was open for 60% of the time, Pallas kernels for 0%

commit v1 on v0

v1 whole, which is shorter than its diff:
```python
import functools

import jax
import jax.numpy as jnp
from jax import lax
from jax.experimental import pallas as pl
from jax.experimental.pallas import tpu as pltpu
from jax.sharding import Mesh, PartitionSpec as P

HEADS = 12
GROUPS = 4
GROUP_HEADS = HEADS // GROUPS
SLAB = 128
Q_BLOCK = 128

epsilon = 1e-06


def gelu_curve(values):
    return jax.nn.gelu(values, approximate=True)


def rms_apply(values, gain_vec):
    factor = lax.rsqrt(jnp.mean(values * values, axis=-1, keepdims=True) + epsilon)
    return (values * factor * gain_vec, factor)


def rms_grad(values, factor, gain_vec, upstream):
    scaled = upstream * gain_vec
    inner_mean = jnp.mean(scaled * values, axis=-1, keepdims=True)
    return (
        factor * scaled - values * factor * factor * factor * inner_mean,
        jnp.sum(upstream * values * factor, axis=0),
    )


def dot_f32(a, b):
    return jnp.dot(a, b, preferred_element_type=jnp.float32)


def exact_dot(a, b):
    return jnp.dot(a, b, precision=lax.Precision.HIGHEST, preferred_element_type=jnp.float32)


def contract(a, b, dims):
    return lax.dot_general(a, b, (dims, ((), ())), preferred_element_type=jnp.float32)


def fill_toeplitz(line_ref, toeplitz):
    base = line_ref[0]
    for step in range(Q_BLOCK // 8):
        rows = base if step == 0 else pltpu.roll(base, 8 * step, 1)
        toeplitz[8 * step : 8 * step + 8, :] = rows


def forward_kernel(keys, blocks, q_ref, kv_ref, line_ref, out_ref, lse_ref, toeplitz):
    block = pl.program_id(1)

    @pl.when(block == 0)
    def _():
        fill_toeplitz(line_ref, toeplitz)

    start = pl.multiple_of((blocks - block) * Q_BLOCK, Q_BLOCK)
    slab = kv_ref[...]
    scores = contract(q_ref[...], slab, ((1,), (1,))) + toeplitz[:, pl.ds(start, keys)]
    top = jnp.max(scores, axis=-1, keepdims=True)
    weights = jnp.exp(scores - top)
    total = jnp.sum(weights, axis=-1, keepdims=True)
    mixed = dot_f32(weights.astype(jnp.bfloat16), slab)
    out_ref[...] = mixed / total
    lse_ref[0] = top + jnp.log(total)


def backward_kernel(
    keys,
    blocks,
    q_ref,
    kv_ref,
    line_ref,
    do_ref,
    out_ref,
    lse_ref,
    dq_ref,
    dkv_ref,
    diag_ref,
    toeplitz,
    folded,
    kv_sum,
):
    block = pl.program_id(1)

    @pl.when(block == 0)
    def _():
        fill_toeplitz(line_ref, toeplitz)
        folded[...] = jnp.zeros_like(folded)

    start = pl.multiple_of((blocks - block) * Q_BLOCK, Q_BLOCK)
    slab = kv_ref[...]
    queries = q_ref[...]
    upstream = do_ref[...]
    scores = contract(queries, slab, ((1,), (1,))) + toeplitz[:, pl.ds(start, keys)]
    probability = jnp.exp(scores - lse_ref[0])
    delta = jnp.sum(upstream.astype(jnp.float32) * out_ref[...], axis=-1, keepdims=True)
    score_grad = probability * (contract(upstream, slab, ((1,), (1,))) - delta)
    low = score_grad.astype(jnp.bfloat16)
    folded[:, pl.ds(start, keys)] += score_grad
    dq_ref[...] = (dot_f32(low, slab) * 0.125).astype(jnp.bfloat16)
    part = contract(low, queries, ((0,), (0,))) + contract(
        probability.astype(jnp.bfloat16), upstream, ((0,), (0,))
    )

    @pl.when(block == 0)
    def _():
        kv_sum[...] = part

    @pl.when(block > 0)
    def _():
        kv_sum[...] += part

    @pl.when(block == blocks - 1)
    def _():
        dkv_ref[...] = kv_sum[...].astype(jnp.bfloat16)
        grid = folded[...]
        width = grid.shape[1]
        half = Q_BLOCK // 2
        while half >= 8:
            grid = grid[:half] + pltpu.roll(grid[half:], width - half, 1)
            half //= 2
        diag_ref[0] = grid


def attention_specs(keys, width):
    return (
        pl.BlockSpec((Q_BLOCK, SLAB), lambda h, b: (b, h)),
        pl.BlockSpec((keys, SLAB), lambda h, b: (0, h)),
        pl.BlockSpec((1, 8, width), lambda h, b: (h, 0, 0)),
        pl.BlockSpec((1, Q_BLOCK, 1), lambda h, b: (h, b, 0)),
    )


def attend(q_slab, kv_slab, lines):
    rows, keys, width = q_slab.shape[0], kv_slab.shape[0], lines.shape[2]
    blocks = rows // Q_BLOCK
    q_spec, kv_spec, line_spec, lse_spec = attention_specs(keys, width)
    return pl.pallas_call(
        functools.partial(forward_kernel, keys, blocks),
        grid=(GROUP_HEADS, blocks),
        in_specs=[q_spec, kv_spec, line_spec],
        out_specs=[q_spec, lse_spec],
        out_shape=[
            jax.ShapeDtypeStruct(q_slab.shape, jnp.float32),
            jax.ShapeDtypeStruct((GROUP_HEADS, rows, 1), jnp.float32),
        ],
        scratch_shapes=[pltpu.VMEM((Q_BLOCK, width), jnp.float32)],
        compiler_params=pltpu.CompilerParams(vmem_limit_bytes=50 * 2**20),
        cost_estimate=pl.CostEstimate(
            flops=4 * rows * keys * SLAB * GROUP_HEADS,
            bytes_accessed=2 * (keys + 3 * rows) * SLAB * GROUP_HEADS,
            transcendentals=rows * keys * GROUP_HEADS,
        ),
        name="attend",
    )(q_slab, kv_slab, lines)


def attend_grad(q_slab, kv_slab, lines, do_slab, out_slab, lse):
    rows, keys, width = q_slab.shape[0], kv_slab.shape[0], lines.shape[2]
    blocks = rows // Q_BLOCK
    q_spec, kv_spec, line_spec, lse_spec = attention_specs(keys, width)
    return pl.pallas_call(
        functools.partial(backward_kernel, keys, blocks),
        grid=(GROUP_HEADS, blocks),
        in_specs=[q_spec, kv_spec, line_spec, q_spec, q_spec, lse_spec],
        out_specs=[q_spec, kv_spec, line_spec],
        out_shape=[
            jax.ShapeDtypeStruct(q_slab.shape, jnp.bfloat16),
            jax.ShapeDtypeStruct(kv_slab.shape, jnp.bfloat16),
            jax.ShapeDtypeStruct(lines.shape, jnp.float32),
        ],
        scratch_shapes=[
            pltpu.VMEM((Q_BLOCK, width), jnp.float32),
            pltpu.VMEM((Q_BLOCK, width), jnp.float32),
            pltpu.VMEM((keys, SLAB), jnp.float32),
        ],
        compiler_params=pltpu.CompilerParams(vmem_limit_bytes=58 * 2**20),
        cost_estimate=pl.CostEstimate(
            flops=10 * rows * keys * SLAB * GROUP_HEADS,
            bytes_accessed=4 * (keys + 3 * rows) * SLAB * GROUP_HEADS,
            transcendentals=rows * keys * GROUP_HEADS,
        ),
        name="attend_grad",
    )(q_slab, kv_slab, lines, do_slab, out_slab, lse)


def assemble_kernel(part_width, whole_ref, qkv_ref, out_ref):
    for matrix in range(4):
        first = matrix * part_width
        rows = jnp.concatenate(
            [
                whole_ref[g][:, first : first + part_width].astype(jnp.float32)
                for g in range(GROUPS)
            ],
            axis=1,
        )
        if matrix < 3:
            qkv_ref[matrix] = rows
        else:
            out_ref[...] = rows


def assemble(whole, part_width):
    row_count, columns = whole.shape[1], whole.shape[2]
    step = 96
    full = part_width * GROUPS
    return pl.pallas_call(
        functools.partial(assemble_kernel, part_width),
        grid=(row_count // step,),
        in_specs=[pl.BlockSpec((GROUPS, step, columns), lambda i: (0, i, 0))],
        out_specs=[
            pl.BlockSpec((3, step, full), lambda i: (0, i, 0)),
            pl.BlockSpec((step, full), lambda i: (i, 0)),
        ],
        out_shape=[
            jax.ShapeDtypeStruct((3, row_count, full), jnp.float32),
            jax.ShapeDtypeStruct((row_count, full), jnp.float32),
        ],
        name="assemble",
    )(whole)


def gather_rows(values, axis):
    return lax.all_gather(values, axis, axis=0, tiled=True)


def scatter_sum(values, axis_name, dim):
    if lax.axis_size(axis_name) != 2:
        return lax.psum_scatter(
            values.astype(jnp.bfloat16), axis_name, scatter_dimension=dim, tiled=True
        ).astype(jnp.float32)
    me = lax.axis_index(axis_name)
    half = values.shape[dim] // 2
    away = lax.dynamic_slice_in_dim(values, (1 - me) * half, half, dim).astype(jnp.bfloat16)
    kept = lax.dynamic_slice_in_dim(values, me * half, half, dim)
    other = lax.ppermute(away, axis_name, [(0, 1), (1, 0)])
    return kept + other.astype(jnp.float32)


def product_shard(left, right):
    if lax.axis_size("fsdp") != 2:
        return scatter_sum(
            jnp.einsum("eca,ecb->eab", left, right, preferred_element_type=jnp.float32), "fsdp", 1
        )
    me = lax.axis_index("fsdp")
    half = left.shape[2] // 2
    away, kept = (
        jnp.einsum(
            "eca,ecb->eab",
            lax.dynamic_slice_in_dim(left, which * half, half, 2),
            right,
            preferred_element_type=jnp.float32,
        )
        for which in (1 - me, me)
    )
    other = lax.ppermute(away.astype(jnp.bfloat16), "fsdp", [(0, 1), (1, 0)])
    return kept + other.astype(jnp.float32)


def per_device(
    tokens,
    qkv_weight,
    out_weight,
    bias_table,
    norm_gain,
    router_weight,
    expert_in,
    expert_out,
    expert_ids,
    slot_ids,
    bucket_table,
    grad_out,
):
    places_axes = ("z", "g")
    group = lax.axis_index("g")
    quarter = lax.axis_index("z")
    row_count = tokens.shape[1]
    model_width = tokens.shape[2]
    head_width = model_width // HEADS
    part_width = model_width // GROUPS
    quarter_rows = row_count * GROUPS
    key_count = quarter_rows * lax.axis_size("z")

    token_rows = tokens[0]
    quarter_tokens = gather_rows(token_rows, "g")
    own_columns = lax.dynamic_slice_in_dim(qkv_weight, group * part_width, part_width, 2)
    qkv_part = lax.all_gather(own_columns, "fsdp", axis=1, tiled=True)
    gain_full = lax.all_gather(norm_gain, "fsdp", axis=1, tiled=True)
    out_full = lax.all_gather(out_weight, "fsdp", axis=0, tiled=True)
    router_full = lax.all_gather(router_weight, "fsdp", axis=0, tiled=True)
    in_full = lax.all_gather(expert_in, "fsdp", axis=1, tiled=True)
    outer_full = lax.all_gather(expert_out, "fsdp", axis=1, tiled=True)

    expert_count = router_full.shape[1]
    capacity = max(2, 2 * row_count // expert_count)
    gains_float = gain_full.astype(jnp.float32)

    centre = (bucket_table.shape[0] - 1) // 2
    width = quarter_rows + key_count
    padded_table = jnp.pad(bucket_table, (1, 0))
    window = lax.dynamic_slice_in_dim(
        padded_table, centre + 1 - quarter_rows - quarter * quarter_rows, width, 0
    )
    bucket_count = bias_table.shape[0]
    marks = (jnp.arange(bucket_count, dtype=jnp.int32)[:, None] == window[None, :]).astype(
        jnp.float32
    )
    own_bias = lax.dynamic_slice_in_dim(bias_table, group * GROUP_HEADS, GROUP_HEADS, 1)
    line = exact_dot(own_bias.T, marks)
    lines = jnp.stack([jnp.roll(line, step, axis=1) for step in range(8)], axis=1)

    quarter_float = quarter_tokens.astype(jnp.float32)
    quarter_normed, quarter_factor = rms_apply(quarter_float, gains_float[0])
    quarter_normed = quarter_normed.astype(jnp.bfloat16)
    weight_heads = qkv_part.reshape(3, model_width, GROUP_HEADS, head_width)
    blank = jnp.zeros_like(weight_heads[0])
    slab_weight = jnp.stack(
        [
            jnp.concatenate([weight_heads[0], blank], axis=-1),
            jnp.concatenate([weight_heads[1], weight_heads[2]], axis=-1),
        ],
        axis=1,
    ).reshape(model_width, 2 * GROUP_HEADS * SLAB)
    projected = dot_f32(quarter_normed, slab_weight).astype(jnp.bfloat16)
    slab_columns = GROUP_HEADS * SLAB
    q_slab = projected[:, :slab_columns] * jnp.bfloat16(0.125)
    kv_slab = gather_rows(projected[:, slab_columns:], "z")
    out_slab, lse = attend(q_slab, kv_slab, lines)
    quarter_out = (
        out_slab.reshape(quarter_rows, GROUP_HEADS, SLAB)[:, :, head_width:]
        .reshape(quarter_rows, part_width)
        .astype(jnp.bfloat16)
    )
    mixed_low = lax.all_to_all(
        quarter_out.reshape(GROUPS, row_count, part_width), "g", 0, 0, tiled=True
    )
    mixed_low = jnp.transpose(mixed_low, (1, 0, 2)).reshape(row_count, model_width)
    quarter_mixed = gather_rows(mixed_low, "g")

    residual = token_rows.astype(jnp.float32)
    middle = residual + dot_f32(mixed_low, out_full)
    normed_two, factor_two = rms_apply(middle, gains_float[1])
    second_low = normed_two.astype(jnp.bfloat16)
    router_prob = jax.nn.softmax(dot_f32(second_low, router_full), axis=-1)
    owner = expert_ids[0]
    chosen = (owner[:, None] == jnp.arange(expert_count, dtype=jnp.int32)[None, :]).astype(
        jnp.float32
    )
    gates = jnp.sum(router_prob * chosen, axis=-1)
    upstream = grad_out[0].astype(jnp.float32)
    target = owner * capacity + slot_ids[0]
    pick = (target[:, None] == jnp.arange(expert_count * capacity, dtype=jnp.int32)).astype(
        jnp.bfloat16
    )

    both = jnp.concatenate([second_low, (gates[:, None] * upstream).astype(jnp.bfloat16)], axis=1)
    send_rows = contract(pick, both, ((0,), (0,))).astype(jnp.bfloat16)
    arrived = lax.all_to_all(send_rows, places_axes, 0, 0, tiled=True)
    place_count = lax.axis_size("z") * GROUPS
    local_count = expert_count // place_count

    def by_expert(rows):
        shaped = rows.reshape(place_count, local_count, capacity, rows.shape[1])
        return jnp.transpose(shaped, (1, 0, 2, 3)).reshape(
            local_count, place_count * capacity, rows.shape[1]
        )

    expert_rows = by_expert(arrived)
    rows_in = expert_rows[:, :, :model_width]
    rows_grad = expert_rows[:, :, model_width:]
    pre_act = jnp.einsum("ecd,edf->ecf", rows_in, in_full, preferred_element_type=jnp.float32)
    active, gelu_pull = jax.vjp(gelu_curve, pre_act)
    active_low = active.astype(jnp.bfloat16)
    produced = jnp.einsum(
        "ecf,efd->ecd", active_low, outer_full, preferred_element_type=jnp.float32
    ).astype(jnp.bfloat16)
    grad_active = jnp.einsum(
        "ecd,efd->ecf", rows_grad, outer_full, preferred_element_type=jnp.float32
    )
    grad_pre = gelu_pull(grad_active)[0].astype(jnp.bfloat16)
    grad_rows = jnp.einsum(
        "ecf,edf->ecd", grad_pre, in_full, preferred_element_type=jnp.float32
    ).astype(jnp.bfloat16)
    leaving = jnp.concatenate([produced, grad_rows], axis=2)
    leaving = jnp.transpose(
        leaving.reshape(local_count, place_count, capacity, 2 * model_width), (1, 0, 2, 3)
    ).reshape(expert_count * capacity, 2 * model_width)
    returned = lax.all_to_all(leaving, places_axes, 0, 0, tiled=True)
    final_outer = product_shard(active_low, rows_grad)
    final_inner = product_shard(rows_in, grad_pre)

    fetched = dot_f32(pick, returned)
    picked = fetched[:, :model_width]
    layer_out = (middle + gates[:, None] * picked).astype(jnp.bfloat16)
    gate_grad = jnp.sum(upstream * picked, axis=-1)
    logit_grad = router_prob * (chosen - gates[:, None]) * gate_grad[:, None]
    router_grad = exact_dot(second_low.astype(jnp.float32).T, logit_grad)
    grad_second = fetched[:, model_width:] + exact_dot(
        logit_grad, router_full.astype(jnp.float32).T
    )
    grad_middle, gain_two_grad = rms_grad(middle, factor_two, gains_float[1], grad_second)
    grad_middle = grad_middle + upstream
    quarter_middle = gather_rows(grad_middle.astype(jnp.bfloat16), "g")

    own_out = lax.dynamic_slice_in_dim(out_full, group * part_width, part_width, 0)
    own_out = own_out.reshape(GROUP_HEADS, head_width, model_width)
    own_out = jnp.concatenate([jnp.zeros_like(own_out), own_out], axis=1).reshape(
        slab_columns, model_width
    )
    do_slab = contract(quarter_middle, own_out, ((1,), (1,))).astype(jnp.bfloat16)
    dq_slab, dkv_part, diag = attend_grad(q_slab, kv_slab, lines, do_slab, out_slab, lse)
    diag_line = sum(jnp.roll(diag[:, step], -step, axis=1) for step in range(8))
    own_table = exact_dot(marks, diag_line.T)
    head_marks = (
        jnp.arange(HEADS, dtype=jnp.int32)[None, :]
        == (group * GROUP_HEADS + jnp.arange(GROUP_HEADS, dtype=jnp.int32))[:, None]
    ).astype(jnp.float32)
    grad_table = exact_dot(own_table, head_marks)
    dkv_parts = lax.all_to_all(dkv_part, "z", 0, 0, tiled=True)
    dkv = (
        jnp.sum(dkv_parts.reshape(-1, quarter_rows, slab_columns).astype(jnp.float32), axis=0)
        .astype(jnp.bfloat16)
    )

    def pick_half(slab, first):
        return slab.reshape(quarter_rows, GROUP_HEADS, SLAB)[
            :, :, first : first + head_width
        ].reshape(quarter_rows, part_width)

    grads_low = jnp.concatenate(
        [pick_half(dq_slab, 0), pick_half(dkv, 0), pick_half(dkv, head_width)], axis=1
    )
    qkv_columns = jnp.transpose(qkv_part, (1, 0, 2)).reshape(model_width, 3 * part_width)
    normed_part = contract(grads_low, qkv_columns, ((1,), (1,)))
    gain_one_part = jnp.sum(normed_part * quarter_float * quarter_factor, axis=0)
    normed_part = normed_part.astype(jnp.bfloat16)
    normed_parts = lax.all_to_all(
        normed_part.reshape(GROUPS, row_count, model_width), "g", 0, 0, tiled=True
    )
    grad_normed = jnp.sum(normed_parts.astype(jnp.float32), axis=0)
    factor_one = lax.rsqrt(jnp.mean(residual * residual, axis=-1, keepdims=True) + epsilon)
    grad_first, _ = rms_grad(residual, factor_one, gains_float[0], grad_normed)
    grad_tokens = (grad_first + grad_middle)[None]

    shard_count = lax.axis_size("fsdp")
    shard_rows = model_width // shard_count
    table_rows = bucket_count // shard_count
    table_column = jnp.pad(
        grad_table.reshape(shard_count, table_rows * HEADS),
        ((0, 0), (0, shard_rows - table_rows * HEADS)),
    ).reshape(model_width)
    small = jnp.concatenate(
        [
            router_grad,
            gain_one_part[:, None],
            gain_two_grad[:, None],
            table_column[:, None],
        ],
        axis=1,
    )
    small = jnp.pad(small, ((0, 0), (0, -small.shape[1] % 128)))
    own_middle = lax.dynamic_slice_in_dim(quarter_middle, group * part_width, part_width, 1)
    dense = jnp.concatenate(
        [
            contract(quarter_normed, grads_low, ((0,), (0,))),
            contract(quarter_mixed, own_middle, ((0,), (0,))),
            small,
        ],
        axis=1,
    )
    columns = dense.shape[1]
    dense = scatter_sum(dense, "fsdp", 0)
    quarter_count = lax.axis_size("z")
    pieces = lax.all_to_all(
        dense.astype(jnp.bfloat16).reshape(quarter_count, -1, columns), "z", 0, 0, tiled=True
    )
    summed = jnp.sum(pieces.astype(jnp.float32), axis=0).astype(jnp.bfloat16)
    whole = gather_rows(gather_rows(summed, "z"), "g").reshape(GROUPS, shard_rows, columns)
    final_qkv, final_out = assemble(whole, part_width)
    totals = jnp.sum(whole[:, :, model_width:].astype(jnp.float32), axis=0)
    table_total = totals[: table_rows * HEADS, expert_count + 2].reshape(table_rows, HEADS)
    return (
        layer_out[None],
        grad_tokens,
        final_qkv,
        final_out,
        table_total,
        totals[:, expert_count : expert_count + 2].T,
        totals[:, :expert_count],
        final_inner,
        final_outer,
    )


def solution(mesh):
    places = ("z", "g")
    devices = mesh.devices.reshape(mesh.shape["ctx"] // GROUPS, GROUPS, mesh.shape["fsdp"])
    finer = Mesh(devices, ("z", "g", "fsdp"))
    placed = (
        P("fsdp", places, None),
        P(None, "fsdp", None),
        P("fsdp", None),
        P(),
        P(None, "fsdp"),
        P("fsdp", None),
        P(places, "fsdp", None),
        P(places, "fsdp", None),
        P("fsdp", places),
        P("fsdp", places),
        P(),
        P("fsdp", places, None),
    )
    return jax.shard_map(
        per_device,
        mesh=finer,
        in_specs=placed,
        out_specs=(
            P("fsdp", places, None),
            P("fsdp", places, None),
            P(None, "fsdp", None),
            P("fsdp", None),
            P("fsdp", None),
            P(None, "fsdp"),
            P("fsdp", None),
            P(places, "fsdp", None),
            P(places, "fsdp", None),
        ),
        check_vma=False,
    )
```

time: 1490 us -> 372 us (0.25)
  local copies, waits for them, and re-layouts: 714 us -> 43.5 us
  blocking collectives: 320 us -> 84.3 us
  matrix products: 158 us -> 66.4 us
  waiting for transfers between devices: 169 us -> 85.9 us
  loops' own time: 39.3 us -> 0 us
  Pallas kernels: 0 us -> 34.5 us
  other arithmetic: 51.6 us -> 18 us
    reshape x20 -> x2, local copies, waits for them, and re-layouts: 235 us -> 1.44 us  [the longest x1 1.38 us: per_device(): grad_table.reshape(shard_count, table_rows * HEADS)]
    psum x1 -> x0, blocking collectives: 204 us -> none  [per_device(): lax.psum((shards[0], shards[1], shards[2], shards[3], shards[4]), 'ctx')]
    another operation x28 -> x11, local copies, waits for them, and re-layouts: 195 us -> 1.44 us  [the longest x1 0.69 us: per_device(): totals[:table_rows * HEADS, expert_count + 2].reshape(table_rows, HEADS)]
    all_gather x8 -> x5, waiting for transfers between devices: 142 us -> 33.4 us  [the longest x2 33.4 us: gather_rows(): return lax.all_gather(values, axis, axis=0, tiled=True)]
    slice x60 -> x28, local copies, waits for them, and re-layouts: 122 us -> 15.3 us  [the longest x14 8.98 us: per_device(): jnp.roll(diag[:, step], -step, axis=1)]
    dot_general x69 -> x22, matrix products: 158 us -> 66.4 us  [the longest x4 25 us: product_shard(): jnp.einsum('eca,ecb->eab', lax.dynamic_slice_in_dim(left, which * half, h...]
    dynamic_slice x44 -> x3, local copies, waits for them, and re-layouts: 51.7 us -> 1.33 us  [the longest x1 0.99 us: per_device(): lax.dynamic_slice_in_dim(out_full, group * part_width, part_width, 0)]
    another operation x3 -> x0, loops' own time: 39.3 us -> none  [by_blocks(): lax.scan(one_turn, carried, (jnp.arange(turn_count, dtype=jnp.int32), res...]
  transfers between devices with their start and end apart: 17 -> 13, of which waited for: 5 -> 6; matrix products, arithmetic and copies ran while one was open for 60% -> 21% of each run, Pallas kernels for 0% -> 3%
where the time goes in v1:
time: 372 us; the launch traced here: 370 us
  waiting for transfers between devices  85.9 us (23%)
  blocking collectives  84.3 us (23%)
  matrix products  66.4 us (18%)
  local copies, waits for them, and re-layouts  43.5 us (12%)
  Pallas kernels  34.5 us (9%)
  starting transfers between devices  23 us (6%)
  other arithmetic  18 us (5%)
  between operations  14.8 us (4%)
    all_gather x4, blocking collectives, gather_rows(): return lax.all_gather(values, axis, axis=0, tiled=True)  54.8 us
    all_gather x2, waiting for transfers between devices, gather_rows(): return lax.all_gather(values, axis, axis=0, tiled=True)  33.4 us
    dot_general x4, matrix products, product_shard(): jnp.einsum('eca,ecb->eab', lax.dynamic_slice_in_dim(left, which * half, h...  25 us
    all_to_all x1, blocking collectives, per_device(): arrived = lax.all_to_all(send_rows, places_axes, 0, 0, tiled=True)  23.3 us
    pallas_call x1, Pallas kernels, attend_grad(): pl.pallas_call(functools.partial(backward_kernel, keys, blocks), grid=(GR...  18.7 us
    all_to_all x1, waiting for transfers between devices, per_device(): returned = lax.all_to_all(leaving, places_axes, 0, 0, tiled=True)  17.2 us
    all_to_all x1, waiting for transfers between devices, per_device(): lax.all_to_all(normed_part.reshape(GROUPS, row_count, model_width), 'g',...  14.4 us
    all_to_all x1, waiting for transfers between devices, per_device(): lax.all_to_all(dense.astype(jnp.bfloat16).reshape(quarter_count, -1, colu...  13.8 us
  transfers between devices with their start and end apart: 13, of which 6 were waited for; matrix products, arithmetic and copies ran while one was open for 21% of the time, Pallas kernels for 3%

profile of v1, /device:TPU:0, one launch (start us, length us, event | category | flops | bytes accessed | tf_op | source)
XLA Modules:
  0.0 370.3 jit_solution(13079130644900775736)
XLA Ops:
  9.2 2.5 all_gather.38
  11.8 13.4 %all-gather = bf16[1,512,768]{2,1,0:T(8,128)(2,1)S(1)} all-gather(bf16[1,128,768]{2,1,0:T(8,128)(2,1)S(1)} %copy-done.19), channel_id=2, replica_groups=mesh['z'=4,'g'=4,'fsdp'=2] {'g'}, dimensions={1}, use_global_device_ids=true | all-gather | bytes 983040 | tf_op jit(solution)/shard_map/all_gather | solution.py:231
  25.3 1.8 all_gather.37
  34.2 1.8 all_gather.41
  36.1 30.7 %all-gather.7.cloned.1.call-done.kv_ref = bf16[2048,384]{1,0:T(8,128)(2,1)} async-done(((bf16[512,384]{1,0:T(8,128)(2,1)}), bf16[2048,384]{1,0:T(8,128)(2,1)}) %all-gather.7.cloned.1.call-update) | async-done | bytes 1572880 | tf_op jit(solution)/shard_map/all_gather | solution.py:231
  68.2 10.8 %attend.1 = (f32[512,384]{1,0:T(8,128)S(1)}, f32[3,512,1]{2,1,0:T(8,128)S(1)}) custom-call(bf16[512,384]{1,0:T(8,128)(2,1)S(1)} %get-tuple-element.55.q_ref, bf16[2048,384]{1,0:T(8,128)(2,1)S(1)} %copy-done.5, f32[3,8,2560]{2,1,0:T(8,128)S(1)} %stack.47.line_ref), custom_call_target="tpu_custom_call" | custom-call | flops 1610612736 | bytes 2752512 | tf_op jit(solution)/shard_map/attend/pallas_call | solution.py:145
  81.0 3.6 all-to-all-start
  84.7 5.1 %all-to-all-done = bf16[4,128,192]{1,2,0:T(8,128)(2,1)S(1)} async-done(((bf16[4,128,192]{1,2,0:T(8,128)(2,1)}), bf16[4,128,192]{1,2,0:T(8,128)(2,1)S(1)}, u32[]{:S(2)}, u32[]{:S(2)}) %all-to-all-start) | async-done | bytes 196640 | tf_op jit(solution)/shard_map/all_to_all | solution.py:341
  89.9 2.0 multiply_reduce_fusion.2
  94.6 23.3 %all_to_all.45 = bf16[16,16,1536]{2,1,0:T(8,128)(2,1)S(1)} all-to-all(bf16[16,16,1536]{2,1,0:T(8,128)(2,1)S(1)} %bitcast.145), channel_id=1, replica_groups=mesh['z'=4,'g'=4,'fsdp'=2] {'z','g'}, dimensions={0} | all-to-all | bytes 1572864 | tf_op jit(solution)/shard_map/all_to_all | solution.py:365
  118.0 8.0 %multiply_convert_fusion = (bf16[2,128,3072]{2,1,0:T(8,128)(2,1)S(1)}, f32[2,128,3072]{2,1,0:T(8,128)}) fusion(bf16[2,768,3072]{2,1,0:T(8,128)(2,1)} %all-gather.11.cloned.1.call-done, bf16[2,128,1536]{2,1,0:T(8,128)(2,1)S(1)} %copy_bitcast_fusion.1), kind=kOutput, calls=%fused_computation.13 | convolution fusion | flops 1215037440 | bytes 14548992 | tf_op jit(solution)/shard_map/ecd,edf->ecf/dot_general | solution.py:378
  126.0 8.4 %fusion.6 = bf16[2,128,3072]{2,1,0:T(8,128)(2,1)S(1)} fusion(f32[2,128,3072]{2,1,0:T(8,128)} %get-tuple-element.69, bf16[2,3072,768]{2,1,0:T(8,128)(2,1)} %all-gather.13.cloned.1.call-done, bf16[2,128,1536]{2,1,0:T(8,128)(2,1)} %copy-done.12), kind=kOutput, calls=%fused_computation.12 | convolution fusion | flops 1223688192 | bytes 14548992 | tf_op jit(solution)/shard_map/ecd,efd->ecf/dot_general | solution.py:384
  134.4 3.4 convolution_convert_fusion.5
  140.5 4.8 %all-to-all-start.2 = ((bf16[16,16,1536]{2,1,0:T(8,128)(2,1)}), bf16[16,16,1536]{2,1,0:T(8,128)(2,1)}, u32[]{:S(2)}, u32[]{:S(2)}) async-start(bf16[16,16,1536]{2,1,0:T(8,128)(2,1)} %copy_bitcast_fusion), calls=%async_computation.2 | async-start | bytes 1572864 | tf_op jit(solution)/shard_map/all_to_all | solution.py:395
  147.2 17.2 %all-to-all-done.2 = bf16[16,16,1536]{2,1,0:T(8,128)(2,1)} async-done(((bf16[16,16,1536]{2,1,0:T(8,128)(2,1)}), bf16[16,16,1536]{2,1,0:T(8,128)(2,1)}, u32[]{:S(2)}, u32[]{:S(2)}) %all-to-all-start.2) | async-done | bytes 786464 | tf_op jit(solution)/shard_map/all_to_all | solution.py:395
  164.5 1.5 fusion.52
  166.0 1.8 fusion.18
  167.9 2.1 multiply_reduce_fusion
  171.9 12.5 %all_gather.44 = bf16[512,768]{1,0:T(8,128)(2,1)S(1)} all-gather(bf16[128,768]{1,0:T(8,128)(2,1)S(1)} %fusion.87), channel_id=1, replica_groups=mesh['z'=4,'g'=4,'fsdp'=2] {'g'}, dimensions={0}, use_global_device_ids=true | all-gather | bytes 983040 | tf_op jit(solution)/shard_map/all_gather | solution.py:231
  186.6 18.7 %attend_grad.1 = (bf16[512,384]{1,0:T(8,128)(2,1)}, bf16[2048,384]{1,0:T(8,128)(2,1)}, f32[3,8,2560]{2,1,0:T(8,128)}) custom-call(bf16[512,384]{1,0:T(8,128)(2,1)} %copy-done.3, bf16[2048,384]{1,0:T(8,128)(2,1)} %all-gather.7.cloned.1.call-done.kv_ref, f32[3,8,2560]{2,1,0:T(8,128)} %copy-done.4, bf16[512,384]{1,0:T(8,128)(2,1)} %convolution_convert_fusion.4.do_ref, ...), custom_call_target="tpu_custom_call" | custom-call | flops 4026531840 | bytes 5505024 | tf_op jit(solution)/shard_map/attend_grad/pallas_call | solution.py:169
  205.3 4.3 %all-to-all-start.3 = ((bf16[4,512,384]{2,1,0:T(8,128)(2,1)}), bf16[4,512,384]{2,1,0:T(8,128)(2,1)}, u32[]{:S(2)}, u32[]{:S(2)}) async-start(bf16[4,512,384]{2,1,0:T(8,128)(2,1)} %bitcast.157), calls=%async_computation.3 | async-start | bytes 3145728 | tf_op jit(solution)/shard_map/all_to_all | solution.py:426
  210.2 11.8 %all_gather.45 = bf16[512,768]{0,1:T(8,128)(2,1)} all-gather(bf16[128,768]{0,1:T(8,128)(2,1)} %bitcast.156), channel_id=1, replica_groups=mesh['z'=4,'g'=4,'fsdp'=2] {'g'}, dimensions={0}, use_global_device_ids=true | all-gather | bytes 983040 | tf_op jit(solution)/shard_map/all_gather | solution.py:231
  233.9 1.9 copy.79
  235.8 1.6 slice.280
  238.6 1.5 fusion.77
  244.1 1.8 fusion.65
  245.9 2.6 fusion.38
  248.5 2.5 reduce_sum.139
  251.0 1.9 copy.80
  254.1 2.0 fusion.40
  256.2 1.7 fusion.11
  258.2 1.5 copy-done.10
  260.6 1.8 slice.276
  262.4 4.8 %convolution_convert_fusion.1 = bf16[2,1536,768]{2,1,0:T(8,128)(2,1)} fusion(bf16[2,128,3072]{2,1,0:T(8,128)(2,1)S(1)} %get-tuple-element.68, s32[]{:T(128)S(6)} %select_n.31, bf16[2,128,1536]{2,1,0:T(8,128)(2,1)} %copy-done.12), kind=kOutput, calls=%fused_computation.3 | convolution fusion | flops 606339072 | bytes 5898244 | tf_op jit(solution)/shard_map/eca,ecb->eab/dot_general | solution.py:255
  267.7 2.1 add_convert_fusion
  269.8 2.2 copy.89
  272.0 5.0 %all-to-all-start.5 = ((bf16[4,96,896]{2,1,0:T(8,128)(2,1)}), bf16[4,96,896]{2,1,0:T(8,128)(2,1)}, u32[]{:S(2)}, u32[]{:S(2)}) async-start(bf16[4,96,896]{2,1,0:T(8,128)(2,1)} %bitcast.153), calls=%async_computation.5 | async-start | bytes 1376256 | tf_op jit(solution)/shard_map/all_to_all | solution.py:481
  277.1 4.5 %convolution_convert_fusion = bf16[2,384,3072]{2,1,0:T(8,128)(2,1)} fusion(bf16[2,128,3072]{2,1,0:T(8,128)(2,1)S(1)} %fusion.6, bf16[2,128,768]{2,1,0:T(8,128)(2,1)} %slice.276, s32[]{:T(128)S(6)} %select_n.29), kind=kOutput, calls=%fused_computation.2 | convolution fusion | flops 606339072 | bytes 6488068 | tf_op jit(solution)/shard_map/eca,ecb->eab/dot_general | solution.py:255
  281.6 13.8 %all-to-all-done.5 = bf16[4,96,896]{2,1,0:T(8,128)(2,1)} async-done(((bf16[4,96,896]{2,1,0:T(8,128)(2,1)}), bf16[4,96,896]{2,1,0:T(8,128)(2,1)}, u32[]{:S(2)}, u32[]{:S(2)}) %all-to-all-start.5) | async-done | bytes 688160 | tf_op jit(solution)/shard_map/all_to_all | solution.py:481
  295.4 1.9 reduce_sum.144
  297.3 17.1 %all_gather.46 = bf16[384,896]{1,0:T(8,128)(2,1)} all-gather(bf16[96,896]{1,0:T(8,128)(2,1)} %reduce_sum.144), channel_id=1, replica_groups=mesh['z'=4,'g'=4,'fsdp'=2] {'z'}, dimensions={0}, use_global_device_ids=true | all-gather | bytes 860160 | tf_op jit(solution)/shard_map/all_gather | solution.py:231
  314.4 4.5 %all-to-all-start.4 = ((bf16[4,128,768]{2,1,0:T(8,128)(2,1)}), bf16[4,128,768]{2,1,0:T(8,128)(2,1)}, u32[]{:S(2)}, u32[]{:S(2)}) async-start(bf16[4,128,768]{2,1,0:T(8,128)(2,1)} %bitcast.166), calls=%async_computation.4 | async-start | bytes 1572864 | tf_op jit(solution)/shard_map/all_to_all | solution.py:444
  318.9 14.4 %all-to-all-done.4 = bf16[4,128,768]{2,1,0:T(8,128)(2,1)} async-done(((bf16[4,128,768]{2,1,0:T(8,128)(2,1)}), bf16[4,128,768]{2,1,0:T(8,128)(2,1)}, u32[]{:S(2)}, u32[]{:S(2)}) %all-to-all-start.4) | async-done | bytes 786464 | tf_op jit(solution)/shard_map/all_to_all | solution.py:444
  334.9 2.2 fusion.25
  337.1 8.0 %convert_add_fusion = f32[2,1536,768]{2,1,0:T(8,128)} fusion(bf16[2,1536,768]{2,1,0:T(8,128)(2,1)} %collective-permute-done.2, bf16[2,128,3072]{2,1,0:T(8,128)(2,1)S(1)} %get-tuple-element.68, s32[]{:T(128)S(6)} %select_n.30, bf16[2,128,1536]{2,1,0:T(8,128)(2,1)S(1)} %copy-done.13), kind=kOutput, calls=%fused_computation | convolution fusion | flops 608698368 | bytes 15335428 | tf_op jit(solution)/shard_map/eca,ecb->eab/dot_general | solution.py:255
  345.1 7.6 %convert_add_fusion.1 = f32[2,384,3072]{2,1,0:T(8,128)} fusion(bf16[2,384,3072]{2,1,0:T(8,128)(2,1)} %collective-permute-done.1, bf16[2,128,3072]{2,1,0:T(8,128)(2,1)S(1)} %fusion.6, bf16[2,128,768]{2,1,0:T(8,128)(2,1)S(1)} %copy-done.24, s32[]{:T(128)S(6)} %select_n.28), kind=kOutput, calls=%fused_computation.1 | convolution fusion | flops 608698368 | bytes 15925252 | tf_op jit(solution)/shard_map/eca,ecb->eab/dot_general | solution.py:255
  352.7 2.6 all-gather.15.cloned.1.call-done
  355.4 4.9 %assemble.1 = (f32[3,384,768]{2,1,0:T(8,128)}, f32[384,768]{1,0:T(8,128)}) custom-call(bf16[4,384,896]{2,1,0:T(8,128)(2,1)} %bitcast.142), custom_call_target="tpu_custom_call" | custom-call | tf_op jit(solution)/shard_map/assemble/pallas_call | solution.py:214
  (237 shorter events, 49.3 us)
Async XLA Ops:
  7.2 4.6 %copy-start.19 = (bf16[1,128,768]{2,1,0:T(8,128)(2,1)S(1)}, bf16[1,128,768]{2,1,0:T(8,128)(2,1)}, u32[]{:S(2)}) copy-start(bf16[1,128,768]{2,1,0:T(8,128)(2,1)} %param.12) | copy-start | bytes 589828
  7.2 59.6 %all-gather.7.cloned.1.call-start = ((), (), s32[]{:S(2)}) async-start(), calls=%async_computation.6 | async-start | bytes 1966080 | tf_op jit(solution)/shard_map/all_gather | solution.py:231
  8.9 16.3 %copy-start.59 = (bf16[2,384]{1,0:T(2,128)(2,1)S(1)}, bf16[2,384]{1,0:T(2,128)(2,1)}, u32[]{:S(2)}) copy-start(bf16[2,384]{1,0:T(2,128)(2,1)} %param.16) | copy-start | bytes 4612
  11.7 15.7 %copy-start.14 = (bf16[3,768,192]{1,2,0:T(8,128)(2,1)}, bf16[3,768,192]{1,2,0:T(8,128)(2,1)S(1)}, u32[]{:S(2)}) copy-start(bf16[3,768,192]{1,2,0:T(8,128)(2,1)S(1)} %all_gather.38) | copy-start | bytes 2654212
  27.1 64.8 %copy-start.32 = (f32[768]{0:T(1024)}, f32[768]{0:T(1024)S(1)}, u32[]{:S(2)}) copy-start(f32[768]{0:T(1024)S(1)} %get-tuple-element.45) | copy-start | bytes 9220
  29.2 37.6 %copy-start.3 = (bf16[512,384]{1,0:T(8,128)(2,1)}, bf16[512,384]{1,0:T(8,128)(2,1)S(1)}, u32[]{:S(2)}) copy-start(bf16[512,384]{1,0:T(8,128)(2,1)S(1)} %get-tuple-element.55.q_ref) | copy-start | bytes 1179652
  29.3 55.5 %all-gather.9.cloned.1.call-start = ((), (), s32[]{:S(2)}) async-start(), calls=%async_computation.7 | async-start | bytes 1769472 | tf_op jit(solution)/shard_map/all_gather | solution.py:296
  30.0 88.0 %all-gather.11.cloned.1.call-start = ((), (), s32[]{:S(2)}) async-start(), calls=%async_computation.8 | async-start | bytes 14155776 | tf_op jit(solution)/shard_map/all_gather | solution.py:298
  30.8 3.5 copy-start.37
  30.8 95.2 %all-gather.13.cloned.1.call-start = ((), (), s32[]{:S(2)}) async-start(), calls=%async_computation.9 | async-start | bytes 14155776 | tf_op jit(solution)/shard_map/all_gather | solution.py:299
  34.2 44.8 %copy-start.4 = (f32[3,8,2560]{2,1,0:T(8,128)}, f32[3,8,2560]{2,1,0:T(8,128)S(1)}, u32[]{:S(2)}) copy-start(f32[3,8,2560]{2,1,0:T(8,128)S(1)} %stack.47.line_ref) | copy-start | bytes 737284
  36.1 56.5 %copy-start.28 = (bf16[768,32]{0,1:T(8,128)(2,1)}, bf16[768,32]{0,1:T(8,128)(2,1)S(1)}, u32[]{:S(2)}) copy-start(bf16[768,32]{0,1:T(8,128)(2,1)S(1)} %all_gather.41) | copy-start | bytes 147460
  80.0 11.9 %copy-start.2 = (f32[512,384]{1,0:T(8,128)}, f32[512,384]{1,0:T(8,128)S(1)}, u32[]{:S(2)}) copy-start(f32[512,384]{1,0:T(8,128)S(1)} %get-tuple-element.16.out_ref) | copy-start | bytes 2359300
  80.0 4.7 %copy-start.52 = (s32[1,128]{1,0:T(1,128)S(1)}, s32[1,128]{1,0:T(1,128)}, u32[]{:S(2)}) copy-start(s32[1,128]{1,0:T(1,128)} %param.20) | copy-start | bytes 1540
  80.0 4.7 %copy-start.60 = (s32[1,128]{1,0:T(1,128)S(1)}, s32[1,128]{1,0:T(1,128)}, u32[]{:S(2)}) copy-start(s32[1,128]{1,0:T(1,128)} %param.21) | copy-start | bytes 1540
  80.0 14.0 %copy-start.20 = (bf16[1,128,768]{2,1,0:T(8,128)(2,1)S(1)}, bf16[1,128,768]{2,1,0:T(8,128)(2,1)}, u32[]{:S(2)}) copy-start(bf16[1,128,768]{2,1,0:T(8,128)(2,1)} %param.23) | copy-start | bytes 589828
  81.0 8.8 %all-to-all-start = ((bf16[4,128,192]{1,2,0:T(8,128)(2,1)}), bf16[4,128,192]{1,2,0:T(8,128)(2,1)S(1)}, u32[]{:S(2)}, u32[]{:S(2)}) async-start(bf16[4,128,192]{1,2,0:T(8,128)(2,1)} %copy.76), calls=%async_computation | async-start | bytes 393216 | tf_op jit(solution)/shard_map/all_to_all | solution.py:341
  84.7 9.9 %copy-start.56 = (s32[128]{0:T(128)}, s32[128]{0:T(128)S(1)}, u32[]{:S(2)}) copy-start(s32[128]{0:T(128)S(1)} %bitcast_add_fusion) | copy-start | bytes 1540
  91.9 26.1 %copy-start.8 = (f32[128,768]{1,0:T(8,128)}, f32[128,768]{1,0:T(8,128)S(1)}, u32[]{:S(2)}) copy-start(f32[128,768]{1,0:T(8,128)S(1)} %get-tuple-element.65) | copy-start | bytes 1179652
  92.6 25.4 %copy-start.21 = (bf16[128,768]{1,0:T(8,128)(2,1)}, bf16[128,768]{1,0:T(8,128)(2,1)S(1)}, u32[]{:S(2)}) copy-start(bf16[128,768]{1,0:T(8,128)(2,1)S(1)} %multiply_convert_fusion.1) | copy-start | bytes 589828
  118.0 8.0 %copy-start.12 = (bf16[2,128,1536]{2,1,0:T(8,128)(2,1)}, bf16[2,128,1536]{2,1,0:T(8,128)(2,1)S(1)}, u32[]{:S(2)}) copy-start(bf16[2,128,1536]{2,1,0:T(8,128)(2,1)S(1)} %copy_bitcast_fusion.1) | copy-start | bytes 2359300
  126.0 8.4 %copy-start.9 = (bf16[2,768,3072]{2,1,0:T(8,128)(2,1)S(1)}, bf16[2,768,3072]{2,1,0:T(8,128)(2,1)}, u32[]{:S(2)}) copy-start(bf16[2,768,3072]{2,1,0:T(8,128)(2,1)} %all-gather.11.cloned.1.call-done) | copy-start | bytes 28311556
  134.4 3.7 copy-start.7
  140.5 23.9 %all-to-all-start.2 = ((bf16[16,16,1536]{2,1,0:T(8,128)(2,1)}), bf16[16,16,1536]{2,1,0:T(8,128)(2,1)}, u32[]{:S(2)}, u32[]{:S(2)}) async-start(bf16[16,16,1536]{2,1,0:T(8,128)(2,1)} %copy_bitcast_fusion), calls=%async_computation.2 | async-start | bytes 1572864 | tf_op jit(solution)/shard_map/all_to_all | solution.py:395
  164.4 3.4 copy-start.40
  164.4 3.4 copy-start.42
  164.4 3.4 copy-start.47
  164.4 3.4 copy-start.49
  164.4 3.4 copy-start.53
  164.5 20.8 %copy-start.27 = (bf16[3,128,768]{2,1,0:T(8,128)(2,1)S(1)}, bf16[3,128,768]{2,1,0:T(8,128)(2,1)}, u32[]{:S(2)}) copy-start(bf16[3,128,768]{2,1,0:T(8,128)(2,1)} %concatenate.91) | copy-start | bytes 1769476
  167.8 16.6 %copy-start.51 = (f32[128]{0:T(128)}, f32[128]{0:T(128)S(1)}, u32[]{:S(2)}) copy-start(f32[128]{0:T(128)S(1)} %get-tuple-element.52) | copy-start | bytes 1540
  170.0 14.4 %copy-start.54 = (f32[128]{0:T(128)}, f32[128]{0:T(128)S(1)}, u32[]{:S(2)}) copy-start(f32[128]{0:T(128)S(1)} %broadcast_multiply_fusion.1) | copy-start | bytes 1540
  205.3 43.2 %all-to-all-start.3 = ((bf16[4,512,384]{2,1,0:T(8,128)(2,1)}), bf16[4,512,384]{2,1,0:T(8,128)(2,1)}, u32[]{:S(2)}, u32[]{:S(2)}) async-start(bf16[4,512,384]{2,1,0:T(8,128)(2,1)} %bitcast.157), calls=%async_computation.3 | async-start | bytes 3145728 | tf_op jit(solution)/shard_map/all_to_all | solution.py:426
  245.9 8.2 %copy-start.36 = (f32[768]{0:T(1024)S(1)}, f32[768]{0:T(1024)}, u32[]{:S(2)}) copy-start(f32[768]{0:T(1024)} %copy-done.35) | copy-start | bytes 9220
  245.9 8.2 %copy-start.58 = (f32[512]{0:T(512)S(1)}, f32[512]{0:T(512)}, u32[]{:S(2)}) copy-start(f32[512]{0:T(512)} %copy-done.57) | copy-start | bytes 6148
  260.6 7.0 %collective-permute-start = (bf16[384,896]{0,1:T(8,128)(2,1)}, bf16[384,896]{0,1:T(8,128)(2,1)}, u32[]{:S(2)}, u32[]{:S(2)}) collective-permute-start(bf16[384,896]{0,1:T(8,128)(2,1)} %dynamic-slice_convert_fusion), channel_id=1, source_target_pairs={{0,1},{1,0},{2,3},{3,2},{4,5},{5,4},{6,7},{7,6},{8,9},{9,8},{10,11... | collective-permute-start | bytes 2064392 | tf_op jit(solution)/shard_map/ppermute | solution.py:243
  262.4 5.3 %copy-start.11 = (f32[768,896]{0,1:T(8,128)S(1)}, f32[768,896]{0,1:T(8,128)}, u32[]{:S(2)}) copy-start(f32[768,896]{0,1:T(8,128)} %copy-done.10) | copy-start | bytes 8257540
  267.2 69.9 %collective-permute-start.2 = (bf16[2,1536,768]{2,1,0:T(8,128)(2,1)}, bf16[2,1536,768]{2,1,0:T(8,128)(2,1)}, u32[]{:S(2)}, u32[]{:S(2)}) collective-permute-start(bf16[2,1536,768]{2,1,0:T(8,128)(2,1)} %convolution_convert_fusion.1), channel_id=1, source_target_pairs={{0,1},{1,0},{2,3},{3,2},{4,5},{5,4},{6,7},{7,6},{8,9},{9,8},{10,11... | collective-permute-start | bytes 14155784 | tf_op jit(solution)/shard_map/ppermute | solution.py:263
  272.0 23.4 %all-to-all-start.5 = ((bf16[4,96,896]{2,1,0:T(8,128)(2,1)}), bf16[4,96,896]{2,1,0:T(8,128)(2,1)}, u32[]{:S(2)}, u32[]{:S(2)}) async-start(bf16[4,96,896]{2,1,0:T(8,128)(2,1)} %bitcast.153), calls=%async_computation.5 | async-start | bytes 1376256 | tf_op jit(solution)/shard_map/all_to_all | solution.py:481
  277.1 78.3 %all-gather.15.cloned.1.call-start = ((), (), s32[]{:S(2)}) async-start(), calls=%async_computation.10 | async-start | bytes 3440640 | tf_op jit(solution)/shard_map/all_gather | solution.py:231
  281.6 53.3 %copy-start.34 = (f32[768]{0:T(1024)S(1)}, f32[768]{0:T(1024)}, u32[]{:S(2)}) copy-start(f32[768]{0:T(1024)} %copy-done.32) | copy-start | bytes 9220
  281.6 53.3 %copy-start.50 = (f32[128]{0:T(128)S(1)}, f32[128]{0:T(128)}, u32[]{:S(2)}) copy-start(f32[128]{0:T(128)} %copy-done.48) | copy-start | bytes 1540
  281.6 53.3 %copy-start.55 = (f32[128]{0:T(128)S(1)}, f32[128]{0:T(128)}, u32[]{:S(2)}) copy-start(f32[128]{0:T(128)} %copy-done.54) | copy-start | bytes 1540
  281.6 63.5 %collective-permute-start.1 = (bf16[2,384,3072]{2,1,0:T(8,128)(2,1)}, bf16[2,384,3072]{2,1,0:T(8,128)(2,1)}, u32[]{:S(2)}, u32[]{:S(2)}) collective-permute-start(bf16[2,384,3072]{2,1,0:T(8,128)(2,1)} %convolution_convert_fusion), channel_id=1, source_target_pairs={{0,1},{1,0},{2,3},{3,2},{4,5},{5,4},{6,7},{7,6},{8,9},{9,8},{10,11... | collective-permute-start | bytes 14155784 | tf_op jit(solution)/shard_map/ppermute | solution.py:263
  314.4 18.9 %all-to-all-start.4 = ((bf16[4,128,768]{2,1,0:T(8,128)(2,1)}), bf16[4,128,768]{2,1,0:T(8,128)(2,1)}, u32[]{:S(2)}, u32[]{:S(2)}) async-start(bf16[4,128,768]{2,1,0:T(8,128)(2,1)} %bitcast.166), calls=%async_computation.4 | async-start | bytes 1572864 | tf_op jit(solution)/shard_map/all_to_all | solution.py:444
  333.3 3.7 %copy-start.13 = (bf16[2,128,1536]{2,1,0:T(8,128)(2,1)S(1)}, bf16[2,128,1536]{2,1,0:T(8,128)(2,1)}, u32[]{:S(2)}) copy-start(bf16[2,128,1536]{2,1,0:T(8,128)(2,1)} %copy-done.12) | copy-start | bytes 2359300
  337.0 8.0 %copy-start.24 = (bf16[2,128,768]{2,1,0:T(8,128)(2,1)S(1)}, bf16[2,128,768]{2,1,0:T(8,128)(2,1)}, u32[]{:S(2)}) copy-start(bf16[2,128,768]{2,1,0:T(8,128)(2,1)} %slice.276) | copy-start | bytes 1179652
  345.1 18.7 %copy-start.1 = (bf16[3,384,768]{2,1,0:T(8,128)(2,1)S(1)}, bf16[3,384,768]{2,1,0:T(8,128)(2,1)}, u32[]{:S(2)}) copy-start(bf16[3,384,768]{2,1,0:T(8,128)(2,1)} %param.13) | copy-start | bytes 5308420
  (26 other events, 44.3 us)
Sparse Core Ops, SparseCore 0:
  29.4 37.3 all-gather.6
  68.4 8.1 all-gather.8
  78.1 21.3 all-gather.10
  100.9 21.3 all-gather.12
  314.5 40.8 all-gather.14

commit v2 on v1

--- a/solution.py
+++ b/solution.py
@@ -244,24 +244,20 @@
     return kept + other.astype(jnp.float32)
 
 
-def product_shard(left, right):
-    if lax.axis_size("fsdp") != 2:
-        return scatter_sum(
-            jnp.einsum("eca,ecb->eab", left, right, preferred_element_type=jnp.float32), "fsdp", 1
-        )
-    me = lax.axis_index("fsdp")
-    half = left.shape[2] // 2
-    away, kept = (
-        jnp.einsum(
-            "eca,ecb->eab",
-            lax.dynamic_slice_in_dim(left, which * half, half, 2),
-            right,
-            preferred_element_type=jnp.float32,
-        )
-        for which in (1 - me, me)
-    )
-    other = lax.ppermute(away.astype(jnp.bfloat16), "fsdp", [(0, 1), (1, 0)])
-    return kept + other.astype(jnp.float32)
+def product_rows(left, right, which):
+    part = left.shape[2] // lax.axis_size("fsdp")
+    return jnp.einsum(
+        "eca,ecb->eab",
+        lax.dynamic_slice_in_dim(left, which * part, part, 2),
+        right,
+        preferred_element_type=jnp.float32,
+    )
+
+
+def product_sum(left, right):
+    return scatter_sum(
+        jnp.einsum("eca,ecb->eab", left, right, preferred_element_type=jnp.float32), "fsdp", 1
+    )
 
 
 def per_device(
@@ -338,11 +334,10 @@
         .reshape(quarter_rows, part_width)
         .astype(jnp.bfloat16)
     )
-    mixed_low = lax.all_to_all(
-        quarter_out.reshape(GROUPS, row_count, part_width), "g", 0, 0, tiled=True
-    )
-    mixed_low = jnp.transpose(mixed_low, (1, 0, 2)).reshape(row_count, model_width)
-    quarter_mixed = gather_rows(mixed_low, "g")
+    quarter_mixed = jnp.transpose(lax.all_gather(quarter_out, "g", axis=0), (1, 0, 2)).reshape(
+        quarter_rows, model_width
+    )
+    mixed_low = lax.dynamic_slice_in_dim(quarter_mixed, group * row_count, row_count, 0)
 
     residual = token_rows.astype(jnp.float32)
     middle = residual + dot_f32(mixed_low, out_full)
@@ -393,8 +388,20 @@
         leaving.reshape(local_count, place_count, capacity, 2 * model_width), (1, 0, 2, 3)
     ).reshape(expert_count * capacity, 2 * model_width)
     returned = lax.all_to_all(leaving, places_axes, 0, 0, tiled=True)
-    final_outer = product_shard(active_low, rows_grad)
-    final_inner = product_shard(rows_in, grad_pre)
+    if lax.axis_size("fsdp") == 2:
+        shard = lax.axis_index("fsdp")
+        away_outer = product_rows(active_low, rows_grad, 1 - shard).astype(jnp.bfloat16)
+        away_inner = product_rows(rows_in, grad_pre, 1 - shard).astype(jnp.bfloat16)
+        returned, away_outer, away_inner = lax.optimization_barrier(
+            (returned, away_outer, away_inner)
+        )
+        other_outer = lax.ppermute(away_outer, "fsdp", [(0, 1), (1, 0)]).astype(jnp.float32)
+        other_inner = lax.ppermute(away_inner, "fsdp", [(0, 1), (1, 0)]).astype(jnp.float32)
+        final_outer = product_rows(active_low, rows_grad, shard) + other_outer
+        final_inner = product_rows(rows_in, grad_pre, shard) + other_inner
+    else:
+        final_outer = product_sum(active_low, rows_grad)
+        final_inner = product_sum(rows_in, grad_pre)
 
     fetched = dot_f32(pick, returned)
     picked = fetched[:, :model_width]

time: 372 us -> 360 us (0.968)
  local copies, waits for them, and re-layouts: 43.5 us -> 31.9 us
  waiting for transfers between devices: 85.9 us -> 91.7 us
  starting transfers between devices: 23 us -> 18.6 us
    all_to_all x1, waiting for transfers between devices: 0.01 us -> 12.1 us  [per_device(): dkv_parts = lax.all_to_all(dkv_part, 'z', 0, 0, tiled=True)]
    all_gather x4 -> x3, blocking collectives: 54.8 us -> 43 us  [gather_rows(): return lax.all_gather(values, axis, axis=0, tiled=True)]
    all_gather x0 -> x1, blocking collectives: none -> 11.2 us  [per_device(): lax.all_gather(quarter_out, 'g', axis=0)]
    all_to_all x1, waiting for transfers between devices: 17.2 us -> 9.38 us  [per_device(): returned = lax.all_to_all(leaving, places_axes, 0, 0, tiled=True)]
    all_to_all x1 -> x0, waiting for transfers between devices: 5.14 us -> none  [per_device(): lax.all_to_all(quarter_out.reshape(GROUPS, row_count, part_width), 'g', 0...]
    all_to_all x1, waiting for transfers between devices: 13.8 us -> 18.4 us  [per_device(): lax.all_to_all(dense.astype(jnp.bfloat16).reshape(quarter_count, -1, colu...]
    unnamed x128 -> x136, local copies, waits for them, and re-layouts: 12.9 us -> 10.1 us
  transfers between devices with their start and end apart: 13 -> 12, of which waited for: 6 -> 7; matrix products, arithmetic and copies ran while one was open for 21% -> 19% of each run, Pallas kernels for 3% -> 3%
where the time goes in v2:
time: 360 us; the launch traced here: 358 us
  waiting for transfers between devices  91.7 us (25%)
  blocking collectives  84.9 us (24%)
  matrix products  65.7 us (18%)
  Pallas kernels  34.5 us (10%)
  local copies, waits for them, and re-layouts  31.9 us (9%)
  starting transfers between devices  18.6 us (5%)
  other arithmetic  16.2 us (4%)
  between operations  14.9 us (4%)
    all_gather x3, blocking collectives, gather_rows(): return lax.all_gather(values, axis, axis=0, tiled=True)  43 us
    all_gather x2, waiting for transfers between devices, gather_rows(): return lax.all_gather(values, axis, axis=0, tiled=True)  32.8 us
    all_to_all x1, blocking collectives, per_device(): arrived = lax.all_to_all(send_rows, places_axes, 0, 0, tiled=True)  24.2 us
    dot_general x4, matrix products, product_rows(): jnp.einsum('eca,ecb->eab', lax.dynamic_slice_in_dim(left, which * part, p...  22.8 us
    pallas_call x1, Pallas kernels, attend_grad(): pl.pallas_call(functools.partial(backward_kernel, keys, blocks), grid=(GR...  18.7 us
    all_to_all x1, waiting for transfers between devices, per_device(): lax.all_to_all(dense.astype(jnp.bfloat16).reshape(quarter_count, -1, colu...  18.4 us
    all_to_all x1, waiting for transfers between devices, per_device(): lax.all_to_all(normed_part.reshape(GROUPS, row_count, model_width), 'g',...  15.2 us
    all_to_all x1, waiting for transfers between devices, per_device(): dkv_parts = lax.all_to_all(dkv_part, 'z', 0, 0, tiled=True)  12.1 us
  transfers between devices with their start and end apart: 12, of which 7 were waited for; matrix products, arithmetic and copies ran while one was open for 19% of the time, Pallas kernels for 3%

profile of v2, /device:TPU:0, one launch (start us, length us, event | category | flops | bytes accessed | tf_op | source)
XLA Modules:
  0.0 358.4 jit_solution(18171866499576097029)
XLA Ops:
  7.3 2.2 all_gather.38
  10.1 2.4 all_gather.39
  12.5 13.5 %all-gather = bf16[1,512,768]{2,1,0:T(8,128)(2,1)S(1)} all-gather(bf16[1,128,768]{2,1,0:T(8,128)(2,1)S(1)} %copy-done.18), channel_id=2, replica_groups=mesh['z'=4,'g'=4,'fsdp'=2] {'g'}, dimensions={1}, use_global_device_ids=true | all-gather | bytes 983040 | tf_op jit(solution)/shard_map/all_gather | solution.py:231
  33.5 1.8 all_gather.43
  35.4 30.7 %all-gather.7.cloned.1.call-done.kv_ref = bf16[2048,384]{1,0:T(8,128)(2,1)} async-done(((bf16[512,384]{1,0:T(8,128)(2,1)}), bf16[2048,384]{1,0:T(8,128)(2,1)}) %all-gather.7.cloned.1.call-update) | async-done | bytes 1572880 | tf_op jit(solution)/shard_map/all_gather | solution.py:231
  66.1 1.4 copy-done.5
  67.5 10.8 %attend.1 = (f32[512,384]{1,0:T(8,128)S(1)}, f32[3,512,1]{2,1,0:T(8,128)S(1)}) custom-call(bf16[512,384]{1,0:T(8,128)(2,1)S(1)} %get-tuple-element.61.q_ref, bf16[2048,384]{1,0:T(8,128)(2,1)S(1)} %copy-done.5, f32[3,8,2560]{2,1,0:T(8,128)S(1)} %stack.47.line_ref), custom_call_target="tpu_custom_call" | custom-call | flops 1610612736 | bytes 2752512 | tf_op jit(solution)/shard_map/attend/pallas_call | solution.py:145
  79.5 11.2 %all_gather.41 = bf16[4,512,192]{1,2,0:T(8,128)(2,1)S(1)} all-gather(bf16[1,512,192]{1,2,0:T(8,128)(2,1)S(1)} %bitcast.165), channel_id=1, replica_groups=mesh['z'=4,'g'=4,'fsdp'=2] {'g'}, dimensions={0}, use_global_device_ids=true | all-gather | bytes 983040 | tf_op jit(solution)/shard_map/all_gather | solution.py:337
  90.8 2.2 multiply_reduce_fusion.2
  95.7 24.2 %all_to_all.40 = bf16[16,16,1536]{2,1,0:T(8,128)(2,1)S(1)} all-to-all(bf16[16,16,1536]{2,1,0:T(8,128)(2,1)S(1)} %bitcast.145), channel_id=1, replica_groups=mesh['z'=4,'g'=4,'fsdp'=2] {'z','g'}, dimensions={0} | all-to-all | bytes 1572864 | tf_op jit(solution)/shard_map/all_to_all | solution.py:360
  120.0 7.7 %multiply_convert_fusion = (bf16[2,128,3072]{2,1,0:T(8,128)(2,1)S(1)}, f32[2,128,3072]{2,1,0:T(8,128)}) fusion(bf16[2,768,3072]{2,1,0:T(8,128)(2,1)} %all-gather.11.cloned.1.call-done, bf16[2,128,1536]{2,1,0:T(8,128)(2,1)S(1)} %copy_bitcast_fusion.1), kind=kOutput, calls=%fused_computation.13 | convolution fusion | flops 1215037440 | bytes 14548992 | tf_op jit(solution)/shard_map/ecd,edf->ecf/dot_general | solution.py:373
  127.7 8.3 %fusion.6 = bf16[2,128,3072]{2,1,0:T(8,128)(2,1)S(1)} fusion(f32[2,128,3072]{2,1,0:T(8,128)} %get-tuple-element.75, bf16[2,3072,768]{2,1,0:T(8,128)(2,1)} %all-gather.13.cloned.1.call-done, bf16[2,128,1536]{2,1,0:T(8,128)(2,1)S(1)} %copy_bitcast_fusion.1), kind=kOutput, calls=%fused_computation.12 | convolution fusion | flops 1223688192 | bytes 14548992 | tf_op jit(solution)/shard_map/ecd,efd->ecf/dot_general | solution.py:379
  136.0 1.5 convolution_convert_fusion.6
  137.5 6.9 %convolution_convert_fusion.5 = bf16[2,128,768]{2,1,0:T(8,128)(2,1)S(1)} fusion(bf16[2,128,3072]{2,1,0:T(8,128)(2,1)S(1)} %fusion.6, bf16[2,768,3072]{2,1,0:T(8,128)(2,1)} %all-gather.11.cloned.1.call-done), kind=kOutput, calls=%fused_computation.29 | convolution fusion | flops 1208156160 | bytes 11403264 | tf_op jit(solution)/shard_map/ecf,edf->ecd/dot_general | solution.py:383
  145.4 4.5 %all-to-all-start.1 = ((bf16[16,16,1536]{2,1,0:T(8,128)(2,1)}), bf16[16,16,1536]{2,1,0:T(8,128)(2,1)}, u32[]{:S(2)}, u32[]{:S(2)}) async-start(bf16[16,16,1536]{2,1,0:T(8,128)(2,1)} %copy_bitcast_fusion), calls=%async_computation.1 | async-start | bytes 1572864 | tf_op jit(solution)/shard_map/all_to_all | solution.py:390
  151.8 3.6 %convolution_convert_fusion.1 = bf16[2,1536,768]{2,1,0:T(8,128)(2,1)} fusion(bf16[2,128,3072]{2,1,0:T(8,128)(2,1)S(1)} %get-tuple-element.74, s32[]{:T(128)S(6)} %select_n.32, bf16[2,128,1536]{2,1,0:T(8,128)(2,1)S(1)} %copy_bitcast_fusion.1), kind=kOutput, calls=%fused_computation.3 | convolution fusion | flops 606339072 | bytes 5898244 | tf_op jit(solution)/shard_map/eca,ecb->eab/dot_general | solution.py:249
  155.4 3.6 %convolution_convert_fusion = bf16[2,384,3072]{2,1,0:T(8,128)(2,1)} fusion(bf16[2,128,3072]{2,1,0:T(8,128)(2,1)S(1)} %copy-done.9, bf16[2,128,768]{2,1,0:T(8,128)(2,1)S(1)} %slice.276, s32[]{:T(128)S(6)} %select_n.33), kind=kOutput, calls=%fused_computation.2 | convolution fusion | flops 606339072 | bytes 6488068 | tf_op jit(solution)/shard_map/eca,ecb->eab/dot_general | solution.py:249
  159.0 9.4 %all-to-all-done.1 = bf16[16,16,1536]{2,1,0:T(8,128)(2,1)} async-done(((bf16[16,16,1536]{2,1,0:T(8,128)(2,1)}), bf16[16,16,1536]{2,1,0:T(8,128)(2,1)}, u32[]{:S(2)}, u32[]{:S(2)}) %all-to-all-start.1) | async-done | bytes 786464 | tf_op jit(solution)/shard_map/all_to_all | solution.py:390
  168.5 1.5 fusion.53
  170.0 1.4 fusion.18
  172.8 12.2 %all_gather.46 = bf16[512,768]{1,0:T(8,128)(2,1)S(1)} all-gather(bf16[128,768]{1,0:T(8,128)(2,1)S(1)} %fusion.89), channel_id=1, replica_groups=mesh['z'=4,'g'=4,'fsdp'=2] {'g'}, dimensions={0}, use_global_device_ids=true | all-gather | bytes 983040 | tf_op jit(solution)/shard_map/all_gather | solution.py:231
  185.9 1.3 convolution_convert_fusion.4.do_ref
  187.3 18.7 %attend_grad.1 = (bf16[512,384]{1,0:T(8,128)(2,1)}, bf16[2048,384]{1,0:T(8,128)(2,1)}, f32[3,8,2560]{2,1,0:T(8,128)}) custom-call(bf16[512,384]{1,0:T(8,128)(2,1)} %copy-done.3, bf16[2048,384]{1,0:T(8,128)(2,1)} %all-gather.7.cloned.1.call-done.kv_ref, f32[3,8,2560]{2,1,0:T(8,128)} %copy-done.4, bf16[512,384]{1,0:T(8,128)(2,1)} %convolution_convert_fusion.4.do_ref, ...), custom_call_target="tpu_custom_call" | custom-call | flops 4026531840 | bytes 5505024 | tf_op jit(solution)/shard_map/attend_grad/pallas_call | solution.py:169
  206.0 4.5 %all-to-all-start.2 = ((bf16[4,512,384]{2,1,0:T(8,128)(2,1)}), bf16[4,512,384]{2,1,0:T(8,128)(2,1)}, u32[]{:S(2)}, u32[]{:S(2)}) async-start(bf16[4,512,384]{2,1,0:T(8,128)(2,1)} %bitcast.155), calls=%async_computation.2 | async-start | bytes 3145728 | tf_op jit(solution)/shard_map/all_to_all | solution.py:433
  221.1 1.9 copy.78
  223.0 1.6 slice.280
  227.4 1.5 fusion.66
  228.9 2.6 fusion.38
  231.5 12.1 %all-to-all-done.2 = bf16[4,512,384]{2,1,0:T(8,128)(2,1)} async-done(((bf16[4,512,384]{2,1,0:T(8,128)(2,1)}), bf16[4,512,384]{2,1,0:T(8,128)(2,1)}, u32[]{:S(2)}, u32[]{:S(2)}) %all-to-all-start.2) | async-done | bytes 1572896 | tf_op jit(solution)/shard_map/all_to_all | solution.py:433
  243.6 2.5 reduce_sum.139
  247.4 2.1 fusion.40
  249.6 1.7 fusion.11
  251.6 1.5 copy-done.11
  254.5 2.0 collective-permute-done
  256.5 2.6 add_convert_fusion
  259.1 2.2 copy.88
  261.3 4.2 %all-to-all-start.4 = ((bf16[4,96,896]{2,1,0:T(8,128)(2,1)}), bf16[4,96,896]{2,1,0:T(8,128)(2,1)}, u32[]{:S(2)}, u32[]{:S(2)}) async-start(bf16[4,96,896]{2,1,0:T(8,128)(2,1)} %bitcast.153), calls=%async_computation.4 | async-start | bytes 1376256 | tf_op jit(solution)/shard_map/all_to_all | solution.py:488
  265.8 18.4 %all-to-all-done.4 = bf16[4,96,896]{2,1,0:T(8,128)(2,1)} async-done(((bf16[4,96,896]{2,1,0:T(8,128)(2,1)}), bf16[4,96,896]{2,1,0:T(8,128)(2,1)}, u32[]{:S(2)}, u32[]{:S(2)}) %all-to-all-start.4) | async-done | bytes 688160 | tf_op jit(solution)/shard_map/all_to_all | solution.py:488
  284.1 1.2 reduce_sum.144
  285.3 17.3 %all_gather.47 = bf16[384,896]{1,0:T(8,128)(2,1)} all-gather(bf16[96,896]{1,0:T(8,128)(2,1)S(1)} %reduce_sum.144), channel_id=1, replica_groups=mesh['z'=4,'g'=4,'fsdp'=2] {'z'}, dimensions={0}, use_global_device_ids=true | all-gather | bytes 860160 | tf_op jit(solution)/shard_map/all_gather | solution.py:231
  302.6 4.5 %all-to-all-start.3 = ((bf16[4,128,768]{2,1,0:T(8,128)(2,1)}), bf16[4,128,768]{2,1,0:T(8,128)(2,1)}, u32[]{:S(2)}, u32[]{:S(2)}) async-start(bf16[4,128,768]{2,1,0:T(8,128)(2,1)} %bitcast.164), calls=%async_computation.3 | async-start | bytes 1572864 | tf_op jit(solution)/shard_map/all_to_all | solution.py:451
  307.1 15.2 %all-to-all-done.3 = bf16[4,128,768]{2,1,0:T(8,128)(2,1)} async-done(((bf16[4,128,768]{2,1,0:T(8,128)(2,1)}), bf16[4,128,768]{2,1,0:T(8,128)(2,1)}, u32[]{:S(2)}, u32[]{:S(2)}) %all-to-all-start.3) | async-done | bytes 786464 | tf_op jit(solution)/shard_map/all_to_all | solution.py:451
  322.3 1.3 convert_reduce_fusion
  323.8 2.0 fusion.25
  325.8 7.9 %convert_add_fusion = f32[2,1536,768]{2,1,0:T(8,128)} fusion(bf16[2,1536,768]{2,1,0:T(8,128)(2,1)} %collective-permute-done.2, bf16[2,128,3072]{2,1,0:T(8,128)(2,1)S(1)} %get-tuple-element.74, s32[]{:T(128)S(6)} %select_n.35, bf16[2,128,1536]{2,1,0:T(8,128)(2,1)S(1)} %copy_bitcast_fusion.1), kind=kOutput, calls=%fused_computation | convolution fusion | flops 608698368 | bytes 15335428 | tf_op jit(solution)/shard_map/eca,ecb->eab/dot_general | solution.py:249
  333.7 7.6 %convert_add_fusion.1 = f32[2,384,3072]{2,1,0:T(8,128)} fusion(bf16[2,384,3072]{2,1,0:T(8,128)(2,1)} %collective-permute-done.1, bf16[2,128,3072]{2,1,0:T(8,128)(2,1)S(1)} %copy-done.10, bf16[2,128,768]{2,1,0:T(8,128)(2,1)S(1)} %copy-done.24, s32[]{:T(128)S(6)} %select_n.34), kind=kOutput, calls=%fused_computation.1 | convolution fusion | flops 608698368 | bytes 15925252 | tf_op jit(solution)/shard_map/eca,ecb->eab/dot_general | solution.py:249
  341.4 2.1 all-gather.15.cloned.1.call-done
  344.8 5.0 %assemble.1 = (f32[3,384,768]{2,1,0:T(8,128)}, f32[384,768]{1,0:T(8,128)}) custom-call(bf16[4,384,896]{2,1,0:T(8,128)(2,1)} %bitcast.143), custom_call_target="tpu_custom_call" | custom-call | tf_op jit(solution)/shard_map/assemble/pallas_call | solution.py:214
  (241 shorter events, 36.9 us)
Async XLA Ops:
  7.2 5.3 %copy-start.18 = (bf16[1,128,768]{2,1,0:T(8,128)(2,1)S(1)}, bf16[1,128,768]{2,1,0:T(8,128)(2,1)}, u32[]{:S(2)}) copy-start(bf16[1,128,768]{2,1,0:T(8,128)(2,1)} %param.12) | copy-start | bytes 589828
  7.2 58.9 %all-gather.7.cloned.1.call-start = ((), (), s32[]{:S(2)}) async-start(), calls=%async_computation.5 | async-start | bytes 1966080 | tf_op jit(solution)/shard_map/all_gather | solution.py:231
  9.5 17.0 %copy-start.35 = (f32[768]{0:T(1024)}, f32[768]{0:T(1024)S(1)}, u32[]{:S(2)}) copy-start(f32[768]{0:T(1024)S(1)} %get-tuple-element.52) | copy-start | bytes 9220
  9.5 83.5 %copy-start.32 = (f32[768]{0:T(1024)}, f32[768]{0:T(1024)S(1)}, u32[]{:S(2)}) copy-start(f32[768]{0:T(1024)S(1)} %get-tuple-element.51) | copy-start | bytes 9220
  12.5 13.9 %copy-start.13 = (bf16[3,768,192]{1,2,0:T(8,128)(2,1)}, bf16[3,768,192]{1,2,0:T(8,128)(2,1)S(1)}, u32[]{:S(2)}) copy-start(bf16[3,768,192]{1,2,0:T(8,128)(2,1)S(1)} %all_gather.39) | copy-start | bytes 2654212
  28.5 37.6 %copy-start.3 = (bf16[512,384]{1,0:T(8,128)(2,1)}, bf16[512,384]{1,0:T(8,128)(2,1)S(1)}, u32[]{:S(2)}) copy-start(bf16[512,384]{1,0:T(8,128)(2,1)S(1)} %get-tuple-element.61.q_ref) | copy-start | bytes 1179652
  28.5 62.2 %all-gather.9.cloned.1.call-start = ((), (), s32[]{:S(2)}) async-start(), calls=%async_computation.6 | async-start | bytes 1769472 | tf_op jit(solution)/shard_map/all_gather | solution.py:292
  29.3 90.7 %all-gather.11.cloned.1.call-start = ((), (), s32[]{:S(2)}) async-start(), calls=%async_computation.7 | async-start | bytes 14155776 | tf_op jit(solution)/shard_map/all_gather | solution.py:294
  30.1 5.3 %copy-start.57 = (s32[1,128]{1,0:T(1,128)S(1)}, s32[1,128]{1,0:T(1,128)}, u32[]{:S(2)}) copy-start(s32[1,128]{1,0:T(1,128)} %param.20) | copy-start | bytes 1540
  30.1 5.3 %copy-start.64 = (s32[1,128]{1,0:T(1,128)S(1)}, s32[1,128]{1,0:T(1,128)}, u32[]{:S(2)}) copy-start(s32[1,128]{1,0:T(1,128)} %param.21) | copy-start | bytes 1540
  30.1 97.6 %all-gather.13.cloned.1.call-start = ((), (), s32[]{:S(2)}) async-start(), calls=%async_computation.8 | async-start | bytes 14155776 | tf_op jit(solution)/shard_map/all_gather | solution.py:295
  30.8 47.5 %copy-start.48 = (s32[2560]{0:T(1024)}, s32[2560]{0:T(1024)S(1)}, u32[]{:S(2)}) copy-start(s32[2560]{0:T(1024)S(1)} %pad_dynamic-slice_fusion) | copy-start | bytes 30724
  33.5 44.9 %copy-start.4 = (f32[3,8,2560]{2,1,0:T(8,128)}, f32[3,8,2560]{2,1,0:T(8,128)S(1)}, u32[]{:S(2)}) copy-start(f32[3,8,2560]{2,1,0:T(8,128)S(1)} %stack.47.line_ref) | copy-start | bytes 737284
  35.4 58.3 %copy-start.28 = (bf16[768,32]{0,1:T(8,128)(2,1)}, bf16[768,32]{0,1:T(8,128)(2,1)S(1)}, u32[]{:S(2)}) copy-start(bf16[768,32]{0,1:T(8,128)(2,1)S(1)} %all_gather.43) | copy-start | bytes 147460
  35.4 59.8 %copy-start.61 = (s32[128]{0:T(128)}, s32[128]{0:T(128)S(1)}, u32[]{:S(2)}) copy-start(s32[128]{0:T(128)S(1)} %bitcast_add_fusion) | copy-start | bytes 1540
  79.3 14.4 %copy-start.2 = (f32[512,384]{1,0:T(8,128)}, f32[512,384]{1,0:T(8,128)S(1)}, u32[]{:S(2)}) copy-start(f32[512,384]{1,0:T(8,128)S(1)} %get-tuple-element.19.out_ref) | copy-start | bytes 2359300
  79.3 15.8 %copy-start.19 = (bf16[1,128,768]{2,1,0:T(8,128)(2,1)S(1)}, bf16[1,128,768]{2,1,0:T(8,128)(2,1)}, u32[]{:S(2)}) copy-start(bf16[1,128,768]{2,1,0:T(8,128)(2,1)} %param.23) | copy-start | bytes 589828
  90.7 29.2 %copy-start.12 = (bf16[4,512,192]{1,2,0:T(8,128)(2,1)}, bf16[4,512,192]{1,2,0:T(8,128)(2,1)S(1)}, u32[]{:S(2)}) copy-start(bf16[4,512,192]{1,2,0:T(8,128)(2,1)S(1)} %all_gather.41) | copy-start | bytes 2359300
  93.7 34.0 %copy-start.20 = (bf16[128,768]{1,0:T(8,128)(2,1)}, bf16[128,768]{1,0:T(8,128)(2,1)S(1)}, u32[]{:S(2)}) copy-start(bf16[128,768]{1,0:T(8,128)(2,1)S(1)} %multiply_convert_fusion.1) | copy-start | bytes 589828
  127.7 8.3 %copy-start.7 = (bf16[2,3072,768]{2,1,0:T(8,128)(2,1)S(1)}, bf16[2,3072,768]{2,1,0:T(8,128)(2,1)}, u32[]{:S(2)}) copy-start(bf16[2,3072,768]{2,1,0:T(8,128)(2,1)} %all-gather.13.cloned.1.call-done) | copy-start | bytes 28311556
  145.4 23.1 %all-to-all-start.1 = ((bf16[16,16,1536]{2,1,0:T(8,128)(2,1)}), bf16[16,16,1536]{2,1,0:T(8,128)(2,1)}, u32[]{:S(2)}, u32[]{:S(2)}) async-start(bf16[16,16,1536]{2,1,0:T(8,128)(2,1)} %copy_bitcast_fusion), calls=%async_computation.1 | async-start | bytes 1572864 | tf_op jit(solution)/shard_map/all_to_all | solution.py:390
  151.8 3.6 %copy-start.23 = (bf16[2,128,768]{2,1,0:T(8,128)(2,1)}, bf16[2,128,768]{2,1,0:T(8,128)(2,1)S(1)}, u32[]{:S(2)}) copy-start(bf16[2,128,768]{2,1,0:T(8,128)(2,1)S(1)} %slice.276) | copy-start | bytes 1179652
  151.8 3.6 %copy-start.9 = (bf16[2,128,3072]{2,1,0:T(8,128)(2,1)S(1)}, bf16[2,128,3072]{2,1,0:T(8,128)(2,1)}, u32[]{:S(2)}) copy-start(bf16[2,128,3072]{2,1,0:T(8,128)(2,1)} %copy-done.8) | copy-start | bytes 4718596
  168.5 17.4 %copy-start.27 = (bf16[3,128,768]{2,1,0:T(8,128)(2,1)S(1)}, bf16[3,128,768]{2,1,0:T(8,128)(2,1)}, u32[]{:S(2)}) copy-start(bf16[3,128,768]{2,1,0:T(8,128)(2,1)} %concatenate.91) | copy-start | bytes 1769476
  171.4 13.6 %copy-start.56 = (f32[128]{0:T(128)}, f32[128]{0:T(128)S(1)}, u32[]{:S(2)}) copy-start(f32[128]{0:T(128)S(1)} %get-tuple-element.58) | copy-start | bytes 1540
  172.6 33.4 %copy-start.15 = (f32[128,768]{1,0:T(8,128)}, f32[128,768]{1,0:T(8,128)S(1)}, u32[]{:S(2)}) copy-start(f32[128,768]{1,0:T(8,128)S(1)} %get-tuple-element.76) | copy-start | bytes 1179652
  172.6 12.4 %copy-start.59 = (f32[128]{0:T(128)}, f32[128]{0:T(128)S(1)}, u32[]{:S(2)}) copy-start(f32[128]{0:T(128)S(1)} %broadcast_multiply_fusion.1) | copy-start | bytes 1540
  205.9 14.6 %copy-start.38 = (f32[768]{0:T(1024)S(1)}, f32[768]{0:T(1024)}, u32[]{:S(2)}) copy-start(f32[768]{0:T(1024)} %get-tuple-element.47) | copy-start | bytes 9220
  205.9 18.7 %copy-start.49 = (s32[2560]{0:T(1024)S(1)}, s32[2560]{0:T(1024)}, u32[]{:S(2)}) copy-start(s32[2560]{0:T(1024)} %copy-done.48) | copy-start | bytes 30724
  206.0 21.4 %copy-start.21 = (bf16[128,768]{1,0:T(8,128)(2,1)S(1)}, bf16[128,768]{1,0:T(8,128)(2,1)}, u32[]{:S(2)}) copy-start(bf16[128,768]{1,0:T(8,128)(2,1)} %copy-done.20) | copy-start | bytes 589828
  206.0 21.4 %copy-start.42 = (f32[128]{0:T(128)S(1)}, f32[128]{0:T(128)}, u32[]{:S(2)}) copy-start(f32[128]{0:T(128)} %copy-done.40) | copy-start | bytes 1540
  206.0 21.4 %copy-start.45 = (f32[128]{0:T(128)S(1)}, f32[128]{0:T(128)}, u32[]{:S(2)}) copy-start(f32[128]{0:T(128)} %copy-done.43) | copy-start | bytes 1540
  206.0 21.4 %copy-start.52 = (f32[128]{0:T(128)S(1)}, f32[128]{0:T(128)}, u32[]{:S(2)}) copy-start(f32[128]{0:T(128)} %copy-done.50) | copy-start | bytes 1540
  206.0 37.6 %all-to-all-start.2 = ((bf16[4,512,384]{2,1,0:T(8,128)(2,1)}), bf16[4,512,384]{2,1,0:T(8,128)(2,1)}, u32[]{:S(2)}, u32[]{:S(2)}) async-start(bf16[4,512,384]{2,1,0:T(8,128)(2,1)} %bitcast.155), calls=%async_computation.2 | async-start | bytes 3145728 | tf_op jit(solution)/shard_map/all_to_all | solution.py:433
  228.9 18.5 %copy-start.36 = (f32[768]{0:T(1024)S(1)}, f32[768]{0:T(1024)}, u32[]{:S(2)}) copy-start(f32[768]{0:T(1024)} %copy-done.35) | copy-start | bytes 9220
  228.9 18.5 %copy-start.63 = (f32[512]{0:T(512)S(1)}, f32[512]{0:T(512)}, u32[]{:S(2)}) copy-start(f32[512]{0:T(512)} %copy-done.62) | copy-start | bytes 6148
  254.0 2.5 collective-permute-start
  254.0 71.8 %collective-permute-start.2 = (bf16[2,1536,768]{2,1,0:T(8,128)(2,1)}, bf16[2,1536,768]{2,1,0:T(8,128)(2,1)}, u32[]{:S(2)}, u32[]{:S(2)}) collective-permute-start(bf16[2,1536,768]{2,1,0:T(8,128)(2,1)} %convolution_convert_fusion.1), channel_id=1, source_target_pairs={{0,1},{1,0},{2,3},{3,2},{4,5},{5,4},{6,7},{7,6},{8,9},{9,8},{10,11... | collective-permute-start | bytes 14155784 | tf_op jit(solution)/shard_map/ppermute | solution.py:398
  261.3 22.8 %all-to-all-start.4 = ((bf16[4,96,896]{2,1,0:T(8,128)(2,1)}), bf16[4,96,896]{2,1,0:T(8,128)(2,1)}, u32[]{:S(2)}, u32[]{:S(2)}) async-start(bf16[4,96,896]{2,1,0:T(8,128)(2,1)} %bitcast.153), calls=%async_computation.4 | async-start | bytes 1376256 | tf_op jit(solution)/shard_map/all_to_all | solution.py:488
  265.5 58.2 %copy-start.34 = (f32[768]{0:T(1024)S(1)}, f32[768]{0:T(1024)}, u32[]{:S(2)}) copy-start(f32[768]{0:T(1024)} %copy-done.32) | copy-start | bytes 9220
  265.5 58.2 %copy-start.55 = (f32[128]{0:T(128)S(1)}, f32[128]{0:T(128)}, u32[]{:S(2)}) copy-start(f32[128]{0:T(128)} %copy-done.53) | copy-start | bytes 1540
  265.5 58.2 %copy-start.60 = (f32[128]{0:T(128)S(1)}, f32[128]{0:T(128)}, u32[]{:S(2)}) copy-start(f32[128]{0:T(128)} %copy-done.59) | copy-start | bytes 1540
  265.5 77.9 %all-gather.15.cloned.1.call-start = ((), (), s32[]{:S(2)}) async-start(), calls=%async_computation.9 | async-start | bytes 3440640 | tf_op jit(solution)/shard_map/all_gather | solution.py:231
  265.6 68.1 %collective-permute-start.1 = (bf16[2,384,3072]{2,1,0:T(8,128)(2,1)}, bf16[2,384,3072]{2,1,0:T(8,128)(2,1)}, u32[]{:S(2)}, u32[]{:S(2)}) collective-permute-start(bf16[2,384,3072]{2,1,0:T(8,128)(2,1)} %convolution_convert_fusion), channel_id=1, source_target_pairs={{0,1},{1,0},{2,3},{3,2},{4,5},{5,4},{6,7},{7,6},{8,9},{9,8},{10,11... | collective-permute-start | bytes 14155784 | tf_op jit(solution)/shard_map/ppermute | solution.py:399
  302.6 19.6 %all-to-all-start.3 = ((bf16[4,128,768]{2,1,0:T(8,128)(2,1)}), bf16[4,128,768]{2,1,0:T(8,128)(2,1)}, u32[]{:S(2)}, u32[]{:S(2)}) async-start(bf16[4,128,768]{2,1,0:T(8,128)(2,1)} %bitcast.164), calls=%async_computation.3 | async-start | bytes 1572864 | tf_op jit(solution)/shard_map/all_to_all | solution.py:451
  325.8 7.9 %copy-start.10 = (bf16[2,128,3072]{2,1,0:T(8,128)(2,1)S(1)}, bf16[2,128,3072]{2,1,0:T(8,128)(2,1)}, u32[]{:S(2)}) copy-start(bf16[2,128,3072]{2,1,0:T(8,128)(2,1)} %copy-done.8) | copy-start | bytes 4718596
  325.8 7.9 %copy-start.24 = (bf16[2,128,768]{2,1,0:T(8,128)(2,1)S(1)}, bf16[2,128,768]{2,1,0:T(8,128)(2,1)}, u32[]{:S(2)}) copy-start(bf16[2,128,768]{2,1,0:T(8,128)(2,1)} %copy-done.23) | copy-start | bytes 1179652
  333.7 18.2 %copy-start.1 = (bf16[3,384,768]{2,1,0:T(8,128)(2,1)S(1)}, bf16[3,384,768]{2,1,0:T(8,128)(2,1)}, u32[]{:S(2)}) copy-start(bf16[3,384,768]{2,1,0:T(8,128)(2,1)} %param.13) | copy-start | bytes 5308420
  (29 other events, 52.4 us)
Sparse Core Ops, SparseCore 0:
  28.7 37.3 all-gather.6
  67.6 8.1 all-gather.8
  77.4 21.3 all-gather.10
  100.2 21.3 all-gather.12
  302.7 40.6 all-gather.14
